TPU v7x, 256 devices: a whole 4x4x8 slice. The times are simulated.
256 devices in a mesh: rep: 8 (over y, core), shard: 32 (over x, z).
Axes of the slice: x: 4, y: 4, z: 8, core: 2. Of those that a mesh axis runs over, the one named last changes fastest.
Arguments:
- tokens: bfloat16 [26624, 2048], P(('rep', 'shard')), may hold values from -6 to 6
- cotangent: bfloat16 [26624, 2048], P(('rep', 'shard')), may hold values from -0.119628906 to 0.119628906
- w_in: bfloat16 [2048, 8192], P(None, 'shard'), may hold values from -0.125 to 0.125
- w_out: bfloat16 [8192, 2048], P('shard'), may hold values from -0.0625 to 0.0625
- momentum: float32 [5, 2097152], P(None, 'shard'), may hold values from -6 to 6
- error: float32 [5, 2097152], P(None, 'shard'), may hold values from -0.3 to 0.3
- block_order: int32 [5, 262144], P(None, 'shard'), may hold values from 0 to 8191, as said below
- signs: int32 [5, 262144], P(None, 'shard'), may hold values from 0 to 1
- heavy_blocks: int32 [8, 2048], P('rep', 'shard'), may hold values from 0 to 8191
- heavy_count: int32 [8, 32], P('rep', 'shard'), may hold values from 1 to 64, as said below
Outputs:
- w_in_new: float32 [2048, 8192], P(None, 'shard')
- w_out_new: float32 [8192, 2048], P('shard')
- momentum_new: float32 [5, 2097152], P(None, 'shard')
- error_new: float32 [5, 2097152], P(None, 'shard')
Inputs may be any that keep to these rules, and one draw needn't show every extreme that they name: `heavy_count`: for each shard exactly one replica has 64 live slots; every other count is at most 16. `block_order`: each row's 8192 entries of one shard are a permutation of 0 to 8191.
All inputs are finite; a program needn't handle non-finite values.
Results may differ from a plain program's by a relative error of at most 0.0028.
Values may be sent and summed in bfloat16 or wider, within the bound.
A program may use at most 192 MiB of HBM per device.

v0:
```python
import jax
import jax.numpy as jnp
from jax import lax
from jax.sharding import PartitionSpec as P

LEARN = 0.05
DECAY = 0.9
ROOT = 0.7978845608028654


def gelu_pair(pre):
    tangent = jnp.tanh(ROOT * (pre + 0.044715 * pre * pre * pre))
    value = 0.5 * pre * (1.0 + tangent)
    slope = 0.5 * (1.0 + tangent) + 0.5 * pre * (1.0 - tangent * tangent) * ROOT * (
        1.0 + 0.134145 * pre * pre
    )
    return (value, slope)


def sketch_part(blocks, offset, order_rows, sign_rows, count):
    local = order_rows - offset
    inside = (local >= 0) & (local < blocks.shape[0])
    factor = jnp.where(inside, jnp.where(sign_rows == 1, 1.0, -1.0), 0.0).astype(jnp.float32)
    picked = blocks[jnp.clip(local, 0, blocks.shape[0] - 1)]
    signed = factor[:, :, None] * picked
    return jnp.sum(signed.reshape(signed.shape[0], count, -1, 128), axis=2)


def middle_value(stack):
    values = [stack[i] for i in range(stack.shape[0])]
    total = len(values)
    for rounds in range(total):
        for i in range(rounds % 2, total - 1, 2):
            lower = jnp.minimum(values[i], values[i + 1])
            upper = jnp.maximum(values[i], values[i + 1])
            values[i] = lower
            values[i + 1] = upper
    return values[total // 2]


def per_device(
    tokens, cotangent, w_in, w_out, momentum, error, block_order, signs, heavy_blocks, heavy_count
):
    rows_count = momentum.shape[0]
    count = momentum.shape[1] // 128
    width = w_in.shape[0]
    cols = w_in.shape[1]
    half = w_in.size // 128
    tok_all, cot_all = (
        lax.all_gather(tokens, "shard", axis=0, tiled=True),
        lax.all_gather(cotangent, "shard", axis=0, tiled=True),
    )
    pre = jnp.dot(tok_all, w_in, preferred_element_type=jnp.float32)
    value, slope = gelu_pair(pre)
    hidden = value.astype(jnp.bfloat16)
    back = lax.dot_general(
        cot_all, w_out, (((1,), (1,)), ((), ())), preferred_element_type=jnp.float32
    )
    pre_grad = (back * slope).astype(jnp.bfloat16)
    grad_out = lax.dot_general(
        hidden, cot_all, (((0,), (0,)), ((), ())), preferred_element_type=jnp.float32
    )
    out_blocks = grad_out.reshape(-1, 128)
    grad_in = lax.dot_general(
        tok_all, pre_grad, (((0,), (0,)), ((), ())), preferred_element_type=jnp.float32
    )
    grads = jnp.concatenate([grad_in.reshape(-1, 128), out_blocks], axis=0)
    table = lax.psum(sketch_part(grads, 0, block_order, signs, count), "rep")
    nblk = grads.shape[0]
    per = nblk // count
    all_lists, all_counts = (
        lax.all_gather(heavy_blocks, "rep", axis=0, tiled=True),
        lax.all_gather(heavy_count, "rep", axis=0, tiled=True),
    )
    slots = all_lists.shape[1]
    flat = all_lists.reshape(-1)
    live = (jnp.arange(slots, dtype=jnp.int32)[None, :] < all_counts).reshape(-1)
    exact = lax.psum(grads[flat], "rep")
    mom = momentum.reshape(rows_count, count, 128)
    err = error.reshape(rows_count, count, 128)
    mom_new = DECAY * mom + table
    probe = err + LEARN * DECAY * mom
    positions = jnp.arange(nblk, dtype=jnp.int32)
    match = block_order[:, None, :] == flat[None, :, None]
    slot = jnp.sum(jnp.where(match, positions[None, None, :], 0), axis=2)
    slot_signs = jnp.take_along_axis(signs, slot, axis=1)
    slot_buckets = slot // per
    factor = jnp.where(slot_signs == 1, 1.0, -1.0).astype(jnp.float32)
    picked = probe[jnp.arange(rows_count, dtype=jnp.int32)[:, None], slot_buckets]
    median = middle_value(picked * factor[:, :, None])
    update = median + LEARN * exact
    total_slots = flat.shape[0]
    order = jnp.arange(total_slots, dtype=jnp.int32)
    earlier = (flat[:, None] == flat[None, :]) & live[None, :] & (order[None, :] < order[:, None])
    keep = live & jnp.logical_not(jnp.any(earlier, axis=1))
    kept_rows = jnp.where(keep[:, None], update, 0.0)
    bucket_ids = jnp.arange(count, dtype=jnp.int32)
    onehot = jnp.where(
        slot_buckets[:, None, :] == bucket_ids[None, :, None], factor[:, None, :], 0.0
    )
    delta_table = jnp.einsum("rcs,sk->rck", onehot, kept_rows, precision=lax.Precision.HIGHEST)
    err_new = err + LEARN * mom_new - delta_table
    target = jnp.where(live, flat, nblk)
    delta = jnp.zeros((nblk, 128), jnp.float32).at[target].set(update, mode="drop")
    w_in_new = w_in.astype(jnp.float32) - delta[:half].reshape(width, cols)
    w_out_new = w_out.astype(jnp.float32) - delta[half:].reshape(cols, width)
    return (
        w_in_new,
        w_out_new,
        mom_new.reshape(rows_count, count * 128),
        err_new.reshape(rows_count, count * 128),
    )


def solution(mesh):
    placed = (
        P(("rep", "shard"), None),
        P(("rep", "shard"), None),
        P(None, "shard"),
        P("shard", None),
        P(None, "shard"),
        P(None, "shard"),
        P(None, "shard"),
        P(None, "shard"),
        P("rep", "shard"),
        P("rep", "shard"),
    )
    return jax.shard_map(
        per_device,
        mesh=mesh,
        in_specs=placed,
        out_specs=(P(None, "shard"), P("shard", None), P(None, "shard"), P(None, "shard")),
        check_vma=False,
    )
```

profile of v0, /device:TPU:1, one launch (start us, length us, event | category | flops | bytes accessed | tf_op | source)
XLA Modules:
  0.0 567.4 jit_solution(12599060822936544704)
XLA Ops:
  11.3 8.8 %all-reduce = s32[8]{0:T(128)S(1)} all-reduce(s32[8]{0:T(128)S(1)} %bitcast_dynamic-update-slice_fusion), channel_id=1, replica_groups=mesh['rep'=8,'shard'=32] {'rep'}, use_global_device_ids=true, to_apply=%add | all-reduce | flops 8 | bytes 64
  20.3 11.9 %all-gather = s32[8,1,64]{2,1,0:T(1,128)S(1)} all-gather(s32[1,1,64]{2,1,0:T(1,128)} %bitcast.78), channel_id=1, replica_groups=mesh['rep'=8,'shard'=32] {'rep'}, dimensions={0}, use_global_device_ids=true | all-gather | bytes 2304 | tf_op jit(solution)/shard_map/all_gather | solution.py:72
  38.2 14.1 %select_reduce_fusion = s32[5,512]{1,0:T(8,128)S(1)} fusion(s32[5,8192]{1,0:T(8,128)S(1)} %copy-done.3, s32[512]{0:T(512)S(1)} %eq.60), kind=kLoop, calls=%fused_computation.5 | loop fusion | flops 62912000 | bytes 176128 | tf_op jit(solution)/shard_map/reduce_sum | solution.py:85
  52.4 1.7 multiply_bitcast_fusion
  56.2 82.6 %all-gather.6.cloned.1.call-done = bf16[3328,2048]{1,0:T(8,128)(2,1)} async-done(((bf16[104,2048]{1,0:T(8,128)(2,1)}), bf16[3328,2048]{1,0:T(8,128)(2,1)}) %all-gather.6.cloned.1.call-update) | async-done | bytes 13631504 | tf_op jit(solution)/shard_map/all_gather | solution.py:50
  138.8 9.1 %fusion.68 = f32[3328,256]{1,0:T(8,128)} fusion(bf16[3328,2048]{1,0:T(8,128)(2,1)} %all-gather.6.cloned.1.call-done, bf16[2048,256]{1,0:T(8,128)(2,1)S(1)} %copy-done.11), kind=kOutput, calls=%fused_computation.114 | convolution fusion | flops 3489660928 | bytes 18087936 | tf_op jit(solution)/shard_map/dot_general | solution.py:53
  147.9 115.1 %all-gather.4.cloned.1.call-done = bf16[3328,2048]{1,0:T(8,128)(2,1)} async-done(((bf16[104,2048]{1,0:T(8,128)(2,1)}), bf16[3328,2048]{1,0:T(8,128)(2,1)}) %all-gather.4.cloned.1.call-update) | async-done | bytes 13631504 | tf_op jit(solution)/shard_map/all_gather | solution.py:51
  263.1 26.4 %fusion.16 = f32[2048,256]{0,1:T(8,128)} fusion(bf16[3328,2048]{1,0:T(8,128)(2,1)} %all-gather.6.cloned.1.call-done, bf16[3328,2048]{1,0:T(8,128)(2,1)} %all-gather.4.cloned.1.call-done, bf16[256,2048]{1,0:T(8,128)(2,1)S(1)} %copy-done.9, f32[3328,256]{1,0:T(8,128)} %fusion.68), kind=kOutput, calls=%fused_computation.27 | convolution fusion | flops 6995509248 | bytes 33816576 | tf_op jit(solution)/shard_map/dot_general | solution.py:64
  289.5 1.9 copy.16
  292.9 3.2 constant_dynamic-update-slice_fusion.1
  296.1 10.2 %fusion.22 = f32[256,2048]{1,0:T(8,128)} fusion(bf16[3328,2048]{1,0:T(8,128)(2,1)} %all-gather.4.cloned.1.call-done, f32[3328,256]{1,0:T(8,128)S(1)} %copy-done.14), kind=kOutput, calls=%fused_computation.39 | convolution fusion | flops 3497328640 | bytes 19136512 | tf_op jit(solution)/shard_map/dot_general | solution.py:60
  306.2 1.7 reshape.270
  309.4 3.9 gather_fusion.1
  313.3 137.3 %gather_fusion.2 = f32[40960,128]{1,0:T(8,128)} fusion(f32[8192,128]{1,0:T(8,128)} %constant_dynamic-update-slice_fusion, s32[40960]{0:T(1024)S(1)} %copy-done.8), kind=kCustom, calls=%fused_computation.2 | custom fusion | bytes 42106880 | tf_op jit(solution)/shard_map/gather | solution.py:24
  450.6 17.3 %multiply_reduce_fusion = f32[5,512,128]{2,1,0:T(8,128)} fusion(f32[5,512,16,128]{3,2,1,0:T(8,128)} %bitcast.71, f32[5,512,16]{2,1,0:T(8,128)S(1)} %copy-done.2), kind=kLoop, calls=%fused_computation.6 | loop fusion | flops 10158080 | bytes 22446080 | tf_op jit(solution)/shard_map/reduce_sum | solution.py:26
  468.8 16.1 %gather_fusion.3 = s32[2560]{0:T(1024)S(1)} fusion(s32[5,8192]{1,0:T(8,128)S(1)} %copy-done, s32[2560]{0:T(1024)S(1)} %reshape.298), kind=kCustom, calls=%fused_computation.3 | custom fusion | bytes 40960 | tf_op jit(solution)/shard_map/jit(take_along_axis)/gather | solution.py:86
  485.0 16.2 %gather_fusion = f32[2560,128]{1,0:T(8,128)S(1)} fusion(f32[5,512,128]{2,1,0:T(8,128)S(1)} %bitcast_add_fusion.1, s32[2560]{0:T(1024)S(1)} %reshape.276), kind=kCustom, calls=%fused_computation | custom fusion | bytes 2641920 | tf_op jit(solution)/shard_map/gather | solution.py:89
  501.6 31.2 %all-reduce.4.cloned.1.call-done = (f32[512,128]{1,0:T(8,128)}, f32[5,512,128]{2,1,0:T(8,128)}) async-done(((f32[512,128]{1,0:T(8,128)}, f32[5,512,128]{2,1,0:T(8,128)}), (f32[512,128]{1,0:T(8,128)}, f32[5,512,128]{2,1,0:T(8,128)})) %all-reduce.4.cloned.1.call-update) | async-done | bytes 1572880 | tf_op jit(solution)/shard_map/psum | solution.py:78
  533.9 3.9 scatter_custom_fusion
  537.8 4.5 fusion.67
  542.3 2.0 reshape.272
  545.9 2.0 reshape.271
  552.2 4.9 fusion.35
  557.1 3.6 copy_bitcast_fusion
  (69 shorter events, 23.0 us)
Async XLA Ops:
  7.2 31.1 %copy-start.3 = (s32[5,8192]{1,0:T(8,128)S(1)}, s32[5,8192]{1,0:T(8,128)}, u32[]{:S(2)}) copy-start(s32[5,8192]{1,0:T(8,128)} %param.16) | copy-start | bytes 491524
  7.2 131.6 %all-gather.6.cloned.1.call-start = ((), (), s32[]{:S(2)}) async-start(), calls=%async_computation.1 | async-start | bytes 14057472 | tf_op jit(solution)/shard_map/all_gather | solution.py:50
  7.9 44.5 %copy-start.4 = (f32[5,65536]{1,0:T(8,128)S(1)}, f32[5,65536]{1,0:T(8,128)}, u32[]{:S(2)}) copy-start(f32[5,65536]{1,0:T(8,128)} %param.14) | copy-start | bytes 3932164
  7.9 255.2 %all-gather.4.cloned.1.call-start = ((), (), s32[]{:S(2)}) async-start(), calls=%async_computation | async-start | bytes 14057472 | tf_op jit(solution)/shard_map/all_gather | solution.py:51
  8.7 524.1 %all-reduce.4.cloned.1.call-start = ((), (), s32[]{:S(2)}) async-start(), calls=%async_computation.2 | async-start | bytes 3145728 | tf_op jit(solution)/shard_map/psum | solution.py:78
  52.4 2.2 copy-start.5
  54.6 0.9 copy-start.13
  54.6 84.2 %copy-start.11 = (bf16[2048,256]{1,0:T(8,128)(2,1)S(1)}, bf16[2048,256]{1,0:T(8,128)(2,1)}, u32[]{:S(2)}) copy-start(bf16[2048,256]{1,0:T(8,128)(2,1)} %param.12) | copy-start | bytes 3145732
  56.2 206.9 %copy-start.9 = (bf16[256,2048]{1,0:T(8,128)(2,1)S(1)}, bf16[256,2048]{1,0:T(8,128)(2,1)}, u32[]{:S(2)}) copy-start(bf16[256,2048]{1,0:T(8,128)(2,1)} %param.13) | copy-start | bytes 3145732
  292.9 3.2 copy-start.14
  309.4 3.9 copy-start.8
  313.3 137.3 %copy-start.2 = (f32[5,512,16]{2,1,0:T(8,128)S(1)}, f32[5,512,16]{2,1,0:T(8,128)}, u32[]{:S(2)}) copy-start(f32[5,512,16]{2,1,0:T(8,128)} %mul.124) | copy-start | bytes 491524
  467.9 0.9 copy-start
  542.3 2.0 copy-start.10
  545.9 2.0 copy-start.12
  547.9 2.4 copy-start.1
  547.9 2.7 copy-start.7
  550.6 1.6 copy-start.6
Sparse Core Ops, SparseCore 0:
  10.6 128.1 all-gather.5
  141.4 121.6 all-gather.3
  468.0 64.7 all-reduce.3
where the time goes:
time: 573 us; the launch traced here: 567 us
  waiting for transfers between devices  230 us (40%)
  local copies, waits for them, and re-layouts  209 us (36%)
  matrix products  50.6 us (9%)
  other arithmetic  42.3 us (7%)
  blocking collectives  20.6 us (4%)
  between operations  14.9 us (3%)
    gather x1, local copies, waits for them, and re-layouts, sketch_part(): picked = blocks[jnp.clip(local, 0, blocks.shape[0] - 1)]  137 us
    all_gather x1, waiting for transfers between devices, per_device(): lax.all_gather(cotangent, 'shard', axis=0, tiled=True)  115 us
    all_gather x1, waiting for transfers between devices, per_device(): lax.all_gather(tokens, 'shard', axis=0, tiled=True)  82.6 us
    psum x1, waiting for transfers between devices, per_device(): exact = lax.psum(grads[flat], 'rep')  31.2 us
    dot_general x1, matrix products, per_device(): lax.dot_general(tok_all, pre_grad, (((0,), (0,)), ((), ())), preferred_el...  26.4 us
    reduce_sum x1, other arithmetic, sketch_part(): return jnp.sum(signed.reshape(signed.shape[0], count, -1, 128), axis=2)  17.3 us
    gather x1, local copies, waits for them, and re-layouts, per_device(): probe[jnp.arange(rows_count, dtype=jnp.int32)[:, None], slot_buckets]  16.2 us
    gather x3, local copies, waits for them, and re-layouts, per_device(): slot_signs = jnp.take_along_axis(signs, slot, axis=1)  16.1 us
  transfers between devices with their start and end apart: 3, of which 3 were waited for; matrix products, arithmetic and copies ran while one was open for 12% of the time, Pallas kernels for 0%

commit v1 on v0

v1 whole, which is shorter than its diff:
```python
import functools

import jax
import jax.numpy as jnp
from jax import lax
from jax.experimental import pallas as pl
from jax.experimental.pallas import tpu as pltpu
from jax.sharding import PartitionSpec as P

MESH = pl.DeviceIdType.MESH
F32, BF16, I32 = jnp.float32, jnp.bfloat16, jnp.int32
LEARN = 0.05
DECAY = 0.9
ROOT = 0.7978845608028654

NX, NY, NZ = 4, 4, 8
TOK = 104
CHIP = 2 * TOK
SUBS = ((0, 112), (112, 96))
DW, COLS = 2048, 256
NB = 8192
COUNT = 512
ROWS = 5
LIVE = 256
TAB = LIVE + ROWS * COUNT
PIECES = ((0, 1280), (1280, 1024), (2304, 512))
CODE = ROWS * 64
META = CODE + 64


def nt(a, b):
    return lax.dot_general(a, b, (((1,), (1,)), ((), ())), preferred_element_type=F32)


def tn(a, b):
    return lax.dot_general(a, b, (((0,), (0,)), ((), ())), preferred_element_type=F32)


def nn(a, b):
    return jnp.dot(a, b, preferred_element_type=F32)


def iota(shape, dim):
    return lax.broadcasted_iota(I32, shape, dim)


def split2(x):
    hi = x.astype(BF16)
    return jnp.concatenate([hi, (x - hi.astype(F32)).astype(BF16)], axis=1)


def place_of(block):
    rest = block - 4096
    return jnp.where(
        block < 4096, (block & 1) * 2048 + (block >> 1), 4096 + (rest & 15) * 256 + (rest >> 4)
    )


def gelu_pair(pre):
    tangent = jnp.tanh(ROOT * (pre + 0.044715 * pre * pre * pre))
    value = 0.5 * pre * (1.0 + tangent)
    slope = 0.5 * (1.0 + tangent) + 0.5 * pre * (1.0 - tangent * tangent) * ROOT * (
        1.0 + 0.134145 * pre * pre
    )
    return value, slope


def invert(ord_ref, sgn_ref, meta_ref):
    step = 1024
    for j in range(ROWS):

        def body(c, acc, j=j):
            at = pl.ds(pl.multiple_of(c * step, step), step)
            place = place_of(ord_ref[j : j + 1, at])
            sign = sgn_ref[j : j + 1, at]
            bucket = (c * step + iota((1, step), 1)) >> 4
            row = iota((128, step), 0)
            value = jnp.where(row < 64, bucket >> 1, (bucket & 1) * 2 + sign)
            left = jnp.where((row & 63) == (place >> 7), value, 0).astype(F32).astype(BF16)
            right = jnp.where(row == (place & 127), 1.0, 0.0).astype(BF16)
            return acc + nt(left, right)

        acc = lax.fori_loop(0, NB // step, body, jnp.zeros((128, 128), F32))
        meta_ref[j * 64 : (j + 1) * 64, :] = (acc[:64] * 4.0 + acc[64:]).astype(I32)


def compact(lists, along):
    full = jnp.concatenate([lists, jnp.zeros((120, 128), I32)], axis=0)
    shape = (LIVE, 128)
    slot, lane = iota(shape, 0), iota(shape, 1)
    wanted = jnp.where(slot < 128, slot & 15, jnp.where(slot < 176, slot - 112, 127))
    pick = jnp.where(lane == wanted, 1.0, 0.0).astype(BF16)
    pick_count = jnp.where(lane == 64, 1.0, 0.0).astype(BF16)
    high = (full >> 7).astype(F32).astype(BF16)
    low = (full & 127).astype(F32).astype(BF16)
    if along == 0:
        values = nt(pick, high) * 128.0 + nt(pick, low)
        counts = nt(pick_count, low)
        spot, rep, axis = slot, lane, 1
    else:
        values = nt(high, pick) * 128.0 + nt(low, pick)
        counts = nt(low, pick_count)
        spot, rep, axis = iota((128, LIVE), 1), iota((128, LIVE), 0), 0
    first = (spot < 128) & (rep == (spot >> 4)) & (counts > (spot & 15).astype(F32))
    later = (spot >= 128) & (spot < 176) & (rep < 8) & (counts > 63.5)
    hit = jnp.where(first | later, 1.0, 0.0)
    live = jnp.sum(hit, axis=axis, keepdims=True)
    block = jnp.sum(hit * values, axis=axis, keepdims=True).astype(I32)
    return jnp.where(live > 0.5, place_of(block), -1)


def lists_of(meta_ref, *lead):
    total = jnp.zeros((8, 128), I32)
    for r in range(8):
        total = total + meta_ref[(*lead, slice(CODE + 8 * r, CODE + 8 * r + 8), slice(None))]
    return total


def middle_value(values):
    values = list(values)
    total = len(values)
    for rounds in range(total):
        for i in range(rounds % 2, total - 1, 2):
            lower = jnp.minimum(values[i], values[i + 1])
            upper = jnp.maximum(values[i], values[i + 1])
            values[i] = lower
            values[i + 1] = upper
    return values[total // 2]


def prepare(meta, momv, errv, medv, infov, acrossv):
    lists = lists_of(meta)
    down, across = compact(lists, 0), compact(lists, 1)
    shape = (LIVE, LIVE)
    same = (down == across) & (across >= 0) & (iota(shape, 1) < iota(shape, 0))
    earlier = jnp.max(jnp.where(same, 1.0, 0.0), axis=1, keepdims=True)
    keep = jnp.where((down >= 0) & (earlier < 0.5), 1, 0)
    codes = meta[...]
    high = (codes >> 2).astype(F32).astype(BF16)
    low = (codes & 3).astype(F32).astype(BF16)
    lane = iota((LIVE, 128), 1)
    lane_hit = lane == (down & 127)
    info = jnp.where(lane == ROWS, keep, 0)
    found = []
    for j in range(ROWS):
        pick = jnp.where(iota((LIVE, META), 1) == (down >> 7) + j * 64, 1.0, 0.0)
        pick = jnp.where(down >= 0, pick, 0.0).astype(BF16)
        value = nn(pick, high) * 4.0 + nn(pick, low)
        code = jnp.sum(jnp.where(lane_hit, value, 0.0), axis=1, keepdims=True).astype(I32)
        info = jnp.where(lane == j, code, info)
        probe = errv[j] + LEARN * DECAY * momv[j]
        got = nn(signed_hit(code), split2(probe))
        found.append(got[:, :128] + got[:, 128:])
    medv[...] = middle_value(found)
    infov[...] = info
    acrossv[...] = jnp.broadcast_to(across, acrossv.shape)


def signed_hit(code):
    sign = jnp.where((code & 1) == 1, 1.0, -1.0)
    return jnp.where(iota((LIVE, COUNT), 1) == (code >> 1), sign, 0.0).astype(BF16)


def main_kernel(
    tok_ref, cot_ref, win_ref, wout_ref, ord_ref, sgn_ref, lst_ref, mom_ref, err_ref,
    ghl_ref, codes_ref, spots_ref, med_ref, info_ref, across_ref,
    own, land, buf, wi, wo, gin, gout, ordv, sgnv, meta, meta2, ghl,
    momv, errv, medv, infov, acrossv, spots,
    lsem, land_sem, ring_s, ring_r, sib_s, sib_r, w_s, w_r, list_s, list_r, meta_s, meta_r,
):
    rep, shard = lax.axis_index("rep"), lax.axis_index("shard")
    y, core = rep // 2, rep % 2
    x, z = shard // NZ, shard % NZ
    other = 1 - core

    def dev(dx=0, dy=0, dz=0, to=None):
        c = core if to is None else to
        return {
            "rep": lax.rem(y + dy + NY, NY) * 2 + c,
            "shard": lax.rem(x + dx + NX, NX) * NZ + lax.rem(z + dz + NZ, NZ),
        }

    def remote(src, dst, send, recv, device):
        return pltpu.make_async_remote_copy(
            src_ref=src, dst_ref=dst, send_sem=send, recv_sem=recv, device_id=device, device_id_type=MESH
        )

    def on_core(c, *actions):
        @pl.when(core == c)
        def _():
            for action in actions:
                action()

    own_tok = pltpu.make_async_copy(tok_ref, own, lsem.at[0])
    own_cot = pltpu.make_async_copy(cot_ref, own, lsem.at[0])
    loads = [
        pltpu.make_async_copy(lst_ref, meta.at[pl.ds(pl.multiple_of(CODE + 8 * rep, 8), 8)], lsem.at[1]),
        pltpu.make_async_copy(ord_ref, ordv, lsem.at[2]),
        pltpu.make_async_copy(sgn_ref, sgnv, lsem.at[3]),
    ]
    tables = [pltpu.make_async_copy(mom_ref.at[:, j, :], momv.at[j], lsem.at[6 + j]) for j in range(ROWS)]
    tables += [pltpu.make_async_copy(err_ref.at[:, j, :], errv.at[j], lsem.at[11 + j]) for j in range(ROWS)]
    own_wi = pltpu.make_async_copy(win_ref, wi.at[:, pl.ds(0, COLS)], lsem.at[4])
    own_wo = pltpu.make_async_copy(wout_ref, wo.at[pl.ds(0, COLS)], lsem.at[5])
    on_core(0, own_tok.start)
    on_core(1, own_cot.start)
    for load in loads:
        load.start()

    barrier = pltpu.get_barrier_semaphore()
    partners = [dev(dz=1), dev(dz=-1)]
    partners += [dev(dx=d, to=c) for d in (1, -1, 2) for c in (0, 1)]
    partners += [dev(dy=d, to=c) for d in (1, 2, 3) for c in (0, 1)] + [dev(to=other)]
    for partner in partners:
        pl.semaphore_signal(barrier, inc=1, device_id=partner, device_id_type=MESH)
    pl.semaphore_wait(barrier, len(partners))

    give_cot = remote(cot_ref, land, land_sem.at[0], land_sem.at[1], dev(to=other))
    give_tok = remote(tok_ref, land, land_sem.at[0], land_sem.at[1], dev(to=other))
    on_core(0, give_cot.start)
    on_core(1, give_tok.start)

    toward = jnp.where(core == 0, -1, 1)
    lower, upper = pl.ds(0, COLS), pl.ds(COLS, COLS)
    landing = pl.ds(pl.multiple_of(other * COLS, COLS), COLS)
    w_in_first = remote(win_ref, wi.at[:, landing], w_s.at[0], w_r.at[0], dev(dx=toward))
    w_out_first = remote(wout_ref, wo.at[landing], w_s.at[1], w_r.at[1], dev(dx=toward))
    w_in_next = remote(wi.at[:, upper], wi.at[:, upper], w_s.at[2], w_r.at[2], dev(dx=-1, to=1))
    w_out_next = remote(wo.at[lower], wo.at[upper], w_s.at[3], w_r.at[3], dev(dx=1, to=1))
    on_core(0, w_in_first.start, w_out_first.start, own_wi.start, own_wo.start)
    on_core(1, w_out_first.start, w_in_first.start)

    loads[0].wait()
    list_row = meta.at[pl.ds(pl.multiple_of(CODE + 8 * rep, 8), 8)]
    peers = [(0, 1), (1, 0), (1, 1), (2, 0), (2, 1), (3, 0), (3, 1)]
    peers = [(n, dev(dy=d, to=other if flip else core)) for n, (d, flip) in enumerate(peers)]
    list_copies = [remote(list_row, list_row, list_s.at[n], list_r.at[n], peer) for n, peer in peers]
    for copy in list_copies:
        copy.start()

    on_core(0, own_tok.wait, give_cot.wait)
    on_core(1, own_cot.wait, give_tok.wait)
    for c in range(4):
        at = slice(c * 512, (c + 1) * 512)
        mine, theirs = own[:, at].astype(F32), land[:, at].astype(F32)
        first, second = jnp.where(core == 0, mine, theirs), jnp.where(core == 0, theirs, mine)
        buf[core, 0:CHIP, at] = jnp.concatenate([first, second], axis=0).astype(BF16)

    def slot_of(way, hops):
        return hops if way == 0 else (NZ - hops) % NZ

    def rows_of(slot, sub):
        return pl.ds(slot * CHIP + SUBS[sub][0], SUBS[sub][1])

    def ring(way, hops, sub):
        return remote(
            buf.at[core, rows_of(slot_of(way, hops), sub)],
            buf.at[core, rows_of(slot_of(way, hops + 1), sub)],
            ring_s.at[way, hops, sub], ring_r.at[way, hops, sub],
            dev(dz=1 if way == 0 else -1),
        )

    def sibling(slot, sub):
        at = buf.at[core, rows_of(slot, sub)]
        return remote(at, at, sib_s.at[slot, sub], sib_r.at[slot, sub], dev(to=other))

    for turn in (0, 1):
        ring(0, 0, turn).start()
        ring(1, 0, 1 - turn).start()
    for sub in (0, 1):
        sibling(0, sub).start()
    for load in tables:
        load.start()

    def arrive(hops, turn):
        for way in (0, 1):
            sub = turn if way == 0 else 1 - turn
            ring(way, hops - 1, sub).wait_recv()
            if hops < 3 or (hops == 3 and turn == 0):
                ring(way, hops, sub).start()
            sibling(slot_of(way, hops), sub).start()

    loads[1].wait()
    loads[2].wait()
    invert(ordv, sgnv, meta)
    for copy in list_copies:
        copy.wait_recv()
    meta_first = remote(meta, meta2.at[other], meta_s.at[0], meta_r.at[0], dev(dx=toward))
    meta_next = remote(meta, meta2.at[1], meta_s.at[1], meta_r.at[1], dev(dx=2))
    meta_first.start()
    on_core(1, meta_next.start)

    @pl.when(core == 0)
    def _():
        meta2[0] = meta[...]

    gin[...] = jnp.zeros_like(gin)
    gout[...] = jnp.zeros_like(gout)

    arrive(1, 0)
    on_core(0, w_in_first.wait_recv, w_in_next.start)
    on_core(1, w_out_first.wait_recv, w_out_next.start)
    arrive(1, 1)
    for load in tables:
        load.wait()
    prepare(meta, momv, errv, medv, infov, acrossv)
    ready = [
        pltpu.make_async_copy(medv, med_ref, lsem.at[16]),
        pltpu.make_async_copy(infov, info_ref, lsem.at[17]),
        pltpu.make_async_copy(acrossv, across_ref, lsem.at[18]),
    ]
    for copy in ready:
        copy.start()
    arrive(2, 0)
    on_core(0, w_out_first.wait_recv, own_wi.wait, own_wo.wait)
    on_core(1, w_in_first.wait_recv)
    arrive(2, 1)
    meta_first.wait_recv()
    on_core(1, meta_next.wait_recv)
    for k in (0, 1):
        spots[k] = jnp.broadcast_to(compact(lists_of(meta2, k), 0), (LIVE, 128))
    ready += [
        pltpu.make_async_copy(meta2, codes_ref, lsem.at[21]),
        pltpu.make_async_copy(spots, spots_ref, lsem.at[22]),
    ]
    for copy in ready[3:]:
        copy.start()
    on_core(1, w_in_next.wait_recv, w_out_next.wait_recv)

    def wait_sibling(slots):
        for slot in slots:
            for sub in (0, 1):
                sibling(slot, sub).wait_recv()

    def work(i, carry):
        @pl.when(i == 0)
        def _():
            wait_sibling((0, 1, 7))

        @pl.when(i == 3)
        def _():
            arrive(3, 0)
            wait_sibling((2, 6))

        @pl.when(i == 5)
        def _():
            arrive(3, 1)
            wait_sibling((3, 5))

        @pl.when(i == 7)
        def _():
            ring(0, 3, 0).wait_recv()
            sibling(4, 0).start()
            ring(1, 3, 1).wait_recv()
            sibling(4, 1).start()
            wait_sibling((4,))

        slot = lax.rem(jnp.where(i % 2 == 1, (i + 1) // 2, NZ - i // 2), NZ)
        rows = pl.ds(pl.multiple_of(slot * CHIP, 16), CHIP)

        value, slope = gelu_pair(nn(buf[0, rows, :], wi[...]))
        back = nt(buf[1, rows, :], wo[...])
        hidden = value.astype(BF16)
        grad = (back * slope).astype(BF16)
        for c in range(4):
            at = slice(c * 512, (c + 1) * 512)
            gin[at, :] += tn(buf[0, rows, at], grad)
            gout[:, at] += tn(hidden, buf[1, rows, at])
        return carry

    lax.fori_loop(0, NZ, work, 0)

    for k in (1, 0):
        for h in range(2):
            at = slice(k * COLS + h * 128, k * COLS + (h + 1) * 128)
            ghl[k, h * 2048 : (h + 1) * 2048, :] = split2(gin[:, at])
        for q in range(16):
            part = gout[k * COLS : (k + 1) * COLS, q * 128 : (q + 1) * 128]
            ghl[k, 4096 + q * 256 : 4352 + q * 256, :] = split2(part)
        ready.append(pltpu.make_async_copy(ghl.at[k], ghl_ref.at[k], lsem.at[19 + k]))
        ready[-1].start()

    for copy in list_copies + [w_in_first, w_out_first, meta_first]:
        copy.wait_send()
    for way in (0, 1):
        for hops in range(4):
            for sub in (0, 1):
                if hops < 3 or sub == way:
                    ring(way, hops, sub).wait_send()
    for slot in range(NZ):
        for sub in (0, 1):
            sibling(slot, sub).wait_send()
    on_core(0, w_in_next.wait_send)
    on_core(1, w_out_next.wait_send, meta_next.wait_send)
    for copy in ready:
        copy.wait()


def sketch_kernel(
    ghl_ref, codes_ref, spots_ref, table_ref,
    ghl, codes, spots, outb, recvx, yb, recvy, tot, lsem, x_s, x_r, y_s, y_r, a_s, a_r,
):
    rep, shard = lax.axis_index("rep"), lax.axis_index("shard")
    y, core = rep // 2, rep % 2
    x, z = shard // NZ, shard % NZ
    other = 1 - core

    def dev(dx=0, dy=0, dz=0, to=None):
        c = core if to is None else to
        return {
            "rep": lax.rem(y + dy + NY, NY) * 2 + c,
            "shard": lax.rem(x + dx + NX, NX) * NZ + lax.rem(z + dz + NZ, NZ),
        }

    def remote(src, dst, send, recv, device):
        return pltpu.make_async_remote_copy(
            src_ref=src, dst_ref=dst, send_sem=send, recv_sem=recv, device_id=device, device_id_type=MESH
        )

    def on_core(c, *actions):
        @pl.when(core == c)
        def _():
            for action in actions:
                action()

    loads = [
        pltpu.make_async_copy(codes_ref, codes, lsem.at[0]),
        pltpu.make_async_copy(spots_ref, spots, lsem.at[1]),
        pltpu.make_async_copy(ghl_ref.at[1], ghl.at[1], lsem.at[2]),
        pltpu.make_async_copy(ghl_ref.at[0], ghl.at[0], lsem.at[3]),
    ]
    for load in loads:
        load.start()
    barrier = pltpu.get_barrier_semaphore()
    partners = [dev(dx=d, to=c) for d in (1, -1, 2) for c in (0, 1)]
    partners += [dev(dy=d, to=c) for d in (1, 2, 3) for c in (0, 1)] + [dev(to=other)]
    for partner in partners:
        pl.semaphore_signal(barrier, inc=1, device_id=partner, device_id_type=MESH)
    pl.semaphore_wait(barrier, len(partners))
    peers = [(0, 1), (1, 0), (1, 1), (2, 0), (2, 1), (3, 0), (3, 1)]
    peers = [(n, dev(dy=d, to=other if flip else core)) for n, (d, flip) in enumerate(peers)]
    loads[0].wait()
    loads[1].wait()

    def one_hot(code, parts):
        ramp = iota((256, 128), 0).astype(F32).astype(BF16)
        code = jnp.broadcast_to(code, (16, 128))
        sign = jnp.where((code & 1) == 1, 1.0, -1.0).astype(BF16)
        bucket = (code >> 1).astype(F32)
        rows = []
        for part in parts:
            spot = (bucket - 256.0 * part).astype(BF16)
            for g in range(16):
                rows.append(jnp.where(spot == ramp[g * 16 : (g + 1) * 16], sign, jnp.zeros_like(sign)))
        return jnp.concatenate(rows, axis=0)

    def sketch(k, left, right, listed):
        step = 8
        parts = left[1]

        def run(*sums):
            def chunk(t, carry):
                tiles = [ghl[k, pl.ds(pl.multiple_of((t * step + i) * 256, 256), 256), :] for i in range(step)]
                found = [codes[k, pl.ds(pl.multiple_of(j * 64 + t * 2 * step, 16), 2 * step), :] for j, _ in (left, right)]
                for unit in (0, 1):
                    pltpu.matmul_push_rhs(tiles[0], 0, unit)
                for i in range(step):
                    if i + 1 < step:
                        for unit in (0, 1):
                            pltpu.matmul_push_rhs(tiles[i + 1], (i + 1) % 2, unit)
                    for unit in (0, 1):
                        code = found[unit][2 * i : 2 * i + 2, :]
                        hot = [one_hot(code[n : n + 1, :], (left, right)[unit][1]) for n in (0, 1)]
                        pltpu.matmul_acc_lhs(sums[unit], jnp.concatenate(hot, axis=1), load_staged_rhs=i % 2)
                        if listed:
                            spot = spots[k, unit * 128 : (unit + 1) * 128, :] - (t * step + i) * 256
                            lane = iota((128, 128), 1)
                            hot = [jnp.where(spot == lane + 128 * n, 1.0, 0.0).astype(BF16) for n in (0, 1)]
                            pltpu.matmul_acc_lhs(sums[2 + unit], jnp.concatenate(hot, axis=1))
                return carry

            lax.fori_loop(0, 32 // step, chunk, 0)
            for unit in (0, 1):
                j, part = (left, right)[unit]
                total = pltpu.matmul_pop(sums[unit])
                start = LIVE + j * COUNT + part[0] * 256
                outb[k, start : start + len(part) * 256, :] = (total[:, :128] + total[:, 128:]).astype(BF16)
                if listed:
                    total = pltpu.matmul_pop(sums[2 + unit])
                    outb[k, unit * 128 : (unit + 1) * 128, :] = (total[:, :128] + total[:, 128:]).astype(BF16)

        rows = [256 * len(parts)] + ([128] if listed else [])
        pl.run_scoped(run, *[pltpu.ACC(mxu_id=unit)((n, 256), F32) for n in rows for unit in (0, 1)])

    def half_of(p):
        return PIECES[p][0] // 2, PIECES[p][1] // 2

    def quarter_of(p):
        return PIECES[p][0] // 8, PIECES[p][1] // 8

    def x_copy(k, p, h, slot, device):
        start, rows = half_of(p)
        return remote(
            outb.at[k, pl.ds(PIECES[p][0] + h * rows, rows)], recvx.at[slot, pl.ds(start, rows)],
            x_s.at[k, p, h], x_r.at[slot, p], device,
        )

    x_far = [[x_copy(1, p, h, 1 + 2 * core, dev(dx=1 + core, to=h)) for h in (0, 1)] for p in range(3)]
    x_near = [[x_copy(0, p, h, 2, dev(dx=-1, to=h)) for h in (0, 1)] for p in range(3)]
    x_home = [x_copy(0, p, 1, 0, dev(to=1)) for p in range(3)]

    def x_far_start(p):
        for copy in x_far[p]:
            copy.start()

    def x_near_start(p):
        start, rows = half_of(p)
        on_core(1, *[copy.start for copy in x_near[p]])

        @pl.when(core == 0)
        def _():
            x_home[p].start()
            recvx[0, start : start + rows, :] = outb[0, PIECES[p][0] : PIECES[p][0] + rows, :]

    def my_quarter(p):
        rows = PIECES[p][1] // 8
        return pl.ds(pl.multiple_of(PIECES[p][0] + core * (4 * rows) + y * rows, 16), rows)

    def y_copy(p, d):
        start, rows = quarter_of(p)
        there = pl.ds(pl.multiple_of(4 * start + lax.rem(y + d, NY) * rows, 16), rows)
        return remote(yb.at[there], recvy.at[d - 1, pl.ds(start, rows)], y_s.at[p, d - 1], y_r.at[p, d - 1], dev(dy=d))

    def y_start(p):
        start, rows = half_of(p)
        on_core(1, x_copy(0, p, 1, 0, dev(to=1)).wait_recv)
        for slot in (1, 2, 3):
            x_copy(1, p, 0, slot, dev(dx=1)).wait_recv()
        part = recvx[0, start : start + rows, :].astype(F32)
        for slot in (1, 2, 3):
            part = part + recvx[slot, start : start + rows, :].astype(F32)
        yb[start : start + rows, :] = part.astype(BF16)
        tot[pl.ds(pl.multiple_of(PIECES[p][0] + core * rows, 16), rows), :] = part
        for d in (1, 2, 3):
            y_copy(p, d).start()

    def a_copy(p, n, peer):
        at = tot.at[my_quarter(p)]
        return remote(at, at, a_s.at[p, n], a_r.at[p, n], peer)

    def a_start(p):
        start, rows = quarter_of(p)
        total = tot[my_quarter(p), :]
        for d in (1, 2, 3):
            y_copy(p, d).wait_recv()
            total = total + recvy[d - 1, start : start + rows, :].astype(F32)
        tot[my_quarter(p), :] = total
        for n, peer in peers:
            a_copy(p, n, peer).start()

    def step(t, carry):
        k = jnp.where(t < 3, 1, 0)
        part = lax.rem(t, 3)

        @pl.when(part == 0)
        def _():
            @pl.when(t == 0)
            def _():
                loads[2].wait()

            @pl.when(t == 3)
            def _():
                loads[3].wait()

            sketch(k, (0, (0, 1)), (1, (0, 1)), True)

        @pl.when(part == 1)
        def _():
            sketch(k, (2, (0, 1)), (3, (0, 1)), False)

        @pl.when(part == 2)
        def _():
            sketch(k, (4, (0,)), (4, (1,)), False)

        for when, action, p in (
            (0, x_far_start, 0), (1, x_far_start, 1), (2, x_far_start, 2),
            (3, x_near_start, 0), (4, x_near_start, 1), (4, y_start, 0), (5, x_near_start, 2), (5, a_start, 0),
            (5, y_start, 1),
        ):

            @pl.when(t == when)
            def _(action=action, p=p):
                action(p)

        return carry

    lax.fori_loop(0, 6, step, 0)
    y_start(2)
    a_start(1)
    a_start(2)
    for p in range(3):
        for n, peer in peers:
            a_copy(p, n, peer).wait_recv()
    result = pltpu.make_async_copy(tot, table_ref, lsem.at[4])
    result.start()

    for p in range(3):
        for copy in x_far[p] + [y_copy(p, d) for d in (1, 2, 3)] + [a_copy(p, n, peer) for n, peer in peers]:
            copy.wait_send()
    on_core(0, *[copy.wait_send for copy in x_home])
    on_core(1, *[c.wait_send for p in range(3) for c in x_near[p]])
    result.wait()


def run_main(tokens, cotangent, w_in, w_out, order, signs, lists, mom, err):
    anywhere = pl.BlockSpec(memory_space=pl.ANY)
    dma = pltpu.SemaphoreType.DMA
    return pl.pallas_call(
        main_kernel,
        out_shape=(
            jax.ShapeDtypeStruct((2, NB, 256), BF16),
            jax.ShapeDtypeStruct((2, META, 128), I32),
            jax.ShapeDtypeStruct((2, LIVE, 128), I32),
            jax.ShapeDtypeStruct((LIVE, 128), F32),
            jax.ShapeDtypeStruct((LIVE, 128), I32),
            jax.ShapeDtypeStruct((8, LIVE), I32),
        ),
        in_specs=[anywhere] * 9,
        out_specs=(anywhere,) * 6,
        scratch_shapes=[
            pltpu.VMEM((TOK, DW), BF16),
            pltpu.VMEM((TOK, DW), BF16),
            pltpu.VMEM((2, NZ * CHIP, DW), BF16),
            pltpu.VMEM((DW, 2 * COLS), BF16),
            pltpu.VMEM((2 * COLS, DW), BF16),
            pltpu.VMEM((DW, 2 * COLS), F32),
            pltpu.VMEM((2 * COLS, DW), F32),
            pltpu.VMEM((ROWS, NB), I32),
            pltpu.VMEM((ROWS, NB), I32),
            pltpu.VMEM((META, 128), I32),
            pltpu.VMEM((2, META, 128), I32),
            pltpu.VMEM((2, NB, 256), BF16),
            pltpu.VMEM((ROWS, COUNT, 128), F32),
            pltpu.VMEM((ROWS, COUNT, 128), F32),
            pltpu.VMEM((LIVE, 128), F32),
            pltpu.VMEM((LIVE, 128), I32),
            pltpu.VMEM((8, LIVE), I32),
            pltpu.VMEM((2, LIVE, 128), I32),
            dma((23,)), dma((2,)),
            dma((2, 4, 2)), dma((2, 4, 2)), dma((NZ, 2)), dma((NZ, 2)), dma((4,)), dma((4,)),
            dma((7,)), dma((7,)), dma((2,)), dma((2,)),
        ],
        compiler_params=pltpu.CompilerParams(
            collective_id=0, has_side_effects=True, vmem_limit_bytes=62 * 1024 * 1024
        ),
        cost_estimate=pl.CostEstimate(flops=15_000_000_000, bytes_accessed=20_000_000, transcendentals=2_000_000),
        name="gather_grad",
    )(tokens, cotangent, w_in, w_out, order, signs, lists, mom, err)


def run_sketch(ghl, codes, spots):
    anywhere = pl.BlockSpec(memory_space=pl.ANY)
    dma = pltpu.SemaphoreType.DMA
    return pl.pallas_call(
        sketch_kernel,
        out_shape=jax.ShapeDtypeStruct((TAB, 128), F32),
        in_specs=[anywhere] * 3,
        out_specs=anywhere,
        scratch_shapes=[
            pltpu.VMEM((2, NB, 256), BF16),
            pltpu.VMEM((2, META, 128), I32),
            pltpu.VMEM((2, LIVE, 128), I32),
            pltpu.VMEM((2, TAB, 128), BF16),
            pltpu.VMEM((4, TAB // 2, 128), BF16),
            pltpu.VMEM((TAB // 2, 128), BF16),
            pltpu.VMEM((3, TAB // 8, 128), BF16),
            pltpu.VMEM((TAB, 128), F32),
            dma((5,)), dma((2, 3, 2)), dma((4, 3)), dma((3, 3)), dma((3, 3)), dma((3, 7)), dma((3, 7)),
        ],
        compiler_params=pltpu.CompilerParams(
            collective_id=1, has_side_effects=True, vmem_limit_bytes=62 * 1024 * 1024
        ),
        cost_estimate=pl.CostEstimate(flops=24_000_000_000, bytes_accessed=10_000_000, transcendentals=0),
        name="sketch_reduce",
    )(ghl, codes, spots)


def finish_kernel(
    table, med, info, across, mom, err, w_in, w_out,
    win_new, wout_new, mom_new, err_new,
    tabv, medv, infov, acrossv, momv, errv, winv, woutv, winn, woutn, momn, errn, sem, out_sem,
):
    pairs = [(info, infov), (med, medv), (table, tabv), (across, acrossv), (w_in, winv), (w_out, woutv)]
    for j in range(ROWS):
        pairs += [(mom.at[:, j, :], momv.at[j]), (err.at[:, j, :], errv.at[j])]
    loads = [pltpu.make_async_copy(src, dst, sem.at[n]) for n, (src, dst) in enumerate(pairs)]
    for load in loads:
        load.start()
    stores = []

    def store(src, dst):
        stores.append(pltpu.make_async_copy(src, dst, out_sem.at[len(stores)]))
        stores[-1].start()

    for load in loads[:4]:
        load.wait()
    codes = infov[...]
    update = medv[...] + LEARN * tabv[:LIVE, :]
    kept = split2(jnp.where(codes[:, ROWS : ROWS + 1] == 1, update, 0.0))
    places = acrossv[0:1, :]

    def delta(start, rows):
        hit = jnp.where(iota((rows, LIVE), 0) + start == places, 1.0, 0.0).astype(BF16)
        got = nn(hit, kept)
        return got[:, :128] + got[:, 128:]

    loads[4].wait()
    for c in range(4):
        rows = pl.ds(c * 512, 512)
        for h in range(2):
            at = slice(h * 128, (h + 1) * 128)
            winn[rows, at] = winv[rows, at].astype(F32) - delta(h * 2048 + c * 512, 512)
        store(winn.at[rows], win_new.at[rows])
    loads[5].wait()
    for c in range(4):
        for q in range(4 * c, 4 * c + 4):
            at = slice(q * 128, (q + 1) * 128)
            woutn[:, at] = woutv[:, at].astype(F32) - delta(4096 + q * 256, 256)
        at = pl.ds(c * 512, 512)
        store(woutn.at[:, at], wout_new.at[:, at])
    for j in range(ROWS):
        loads[6 + 2 * j].wait()
        loads[7 + 2 * j].wait()
        fresh = DECAY * momv[j] + tabv[LIVE + j * COUNT : LIVE + (j + 1) * COUNT, :]
        momn[j] = fresh
        store(momn.at[j], mom_new.at[:, j, :])
        gone = tn(signed_hit(codes[:, j : j + 1]), kept)
        errn[j] = errv[j] + LEARN * fresh - (gone[:, :128] + gone[:, 128:])
        store(errn.at[j], err_new.at[:, j, :])
    for copy in stores:
        copy.wait()


def run_finish(table, med, info, across, mom, err, w_in, w_out):
    anywhere = pl.BlockSpec(memory_space=pl.ANY)
    vmem = pltpu.VMEM
    deep = vmem((ROWS, COUNT, 128), F32)
    return pl.pallas_call(
        finish_kernel,
        out_shape=(
            jax.ShapeDtypeStruct(w_in.shape, F32),
            jax.ShapeDtypeStruct(w_out.shape, F32),
            jax.ShapeDtypeStruct(mom.shape, F32),
            jax.ShapeDtypeStruct(err.shape, F32),
        ),
        in_specs=[anywhere] * 8,
        out_specs=(anywhere,) * 4,
        scratch_shapes=[
            vmem((TAB, 128), F32), vmem((LIVE, 128), F32), vmem((LIVE, 128), I32), vmem((8, LIVE), I32),
            deep, deep, vmem(w_in.shape, BF16), vmem(w_out.shape, BF16), vmem(w_in.shape, F32), vmem(w_out.shape, F32),
            deep, deep, pltpu.SemaphoreType.DMA((16,)), pltpu.SemaphoreType.DMA((18,)),
        ],
        compiler_params=pltpu.CompilerParams(vmem_limit_bytes=62 * 1024 * 1024),
        cost_estimate=pl.CostEstimate(flops=3_000_000_000, bytes_accessed=16_000_000, transcendentals=0),
        name="finish",
    )(table, med, info, across, mom, err, w_in, w_out)


def per_device(
    tokens, cotangent, w_in, w_out, momentum, error, block_order, signs, heavy_blocks, heavy_count
):
    listed = jnp.concatenate([heavy_blocks, jnp.broadcast_to(heavy_count, heavy_blocks.shape)], axis=1)
    here = lax.broadcasted_iota(I32, (8, 128), 0) == lax.axis_index("rep")
    lists = jnp.where(here, listed, 0)
    mom, err = by_bucket(momentum), by_bucket(error)
    ghl, codes, spots, med, info, across = run_main(
        tokens, cotangent, w_in, w_out, block_order, signs, lists, mom, err
    )
    table = run_sketch(ghl, codes, spots)
    win_new, wout_new, mom_new, err_new = run_finish(table, med, info, across, mom, err, w_in, w_out)
    return win_new, wout_new, by_row(mom_new), by_row(err_new)


def by_bucket(table):
    return jnp.transpose(table.reshape(ROWS, COUNT, 128), (1, 0, 2))


def by_row(table):
    return jnp.transpose(table, (1, 0, 2)).reshape(ROWS, COUNT * 128)


def solution(mesh):
    placed = (
        P(("rep", "shard"), None),
        P(("rep", "shard"), None),
        P(None, "shard"),
        P("shard", None),
        P(None, "shard"),
        P(None, "shard"),
        P(None, "shard"),
        P(None, "shard"),
        P("rep", "shard"),
        P("rep", "shard"),
    )
    return jax.shard_map(
        per_device,
        mesh=mesh,
        in_specs=placed,
        out_specs=(P(None, "shard"), P("shard", None), P(None, "shard"), P(None, "shard")),
        check_vma=False,
    )
```

time: 573 us -> 152 us (0.27)
  waiting for transfers between devices: 230 us -> 0 us
  local copies, waits for them, and re-layouts: 209 us -> 0.66 us
  Pallas kernels: 0 us -> 149 us
  matrix products: 50.6 us -> 0 us
  other arithmetic: 42.3 us -> 0.67 us
  blocking collectives: 20.6 us -> 0 us
  between operations: 14.9 us -> 1.46 us
    all_gather x2 -> x0, waiting for transfers between devices: 198 us -> none  [the longest x1 115 us: per_device(): lax.all_gather(cotangent, 'shard', axis=0, tiled=True)]
    gather x6 -> x0, local copies, waits for them, and re-layouts: 173 us -> none  [the longest x1 137 us: sketch_part(): picked = blocks[jnp.clip(local, 0, blocks.shape[0] - 1)]]
    pallas_call x0 -> x3, Pallas kernels: none -> 149 us  [the longest x1 87.3 us: run_main(): pl.pallas_call(main_kernel, out_shape=(jax.ShapeDtypeStruct((2, NB, 256),...]
    dot_general x4 -> x0, matrix products: 50.6 us -> none  [the longest x1 26.4 us: per_device(): lax.dot_general(tok_all, pre_grad, (((0,), (0,)), ((), ())), preferred_el...]
    reduce_sum x2 -> x0, other arithmetic: 31.4 us -> none  [the longest x1 17.3 us: sketch_part(): return jnp.sum(signed.reshape(signed.shape[0], count, -1, 128), axis=2)]
    psum x1 -> x0, waiting for transfers between devices: 31.2 us -> none  [per_device(): exact = lax.psum(grads[flat], 'rep')]
    all_gather x1 -> x0, blocking collectives: 11.9 us -> none  [per_device(): lax.all_gather(heavy_blocks, 'rep', axis=0, tiled=True)]
    reshape x6 -> x0, local copies, waits for them, and re-layouts: 10.7 us -> none  [the longest x1 3.56 us: per_device(): err_new.reshape(rows_count, count * 128)]
  transfers between devices with their start and end apart: 3 -> 0, of which waited for: 3 -> 0; matrix products, arithmetic and copies ran while one was open for 12% -> 0% of each run, Pallas kernels for 0% -> 0%
where the time goes in v1:
time: 152 us
  Pallas kernels  149 us (98%)
    pallas_call x1, Pallas kernels, run_main(): pl.pallas_call(main_kernel, out_shape=(jax.ShapeDtypeStruct((2, NB, 256),...  87.3 us
    pallas_call x1, Pallas kernels, run_sketch(): pl.pallas_call(sketch_kernel, out_shape=jax.ShapeDtypeStruct((TAB, 128),...  55.4 us
    pallas_call x1, Pallas kernels, run_finish(): pl.pallas_call(finish_kernel, out_shape=(jax.ShapeDtypeStruct(w_in.shape,...  6.42 us

profile of v1, /device:TPU:1, one launch (start us, length us, event | category | flops | bytes accessed | tf_op | source)
XLA Modules:
  0.0 151.9 jit_solution(9180458698386653544)
XLA Ops:
  1.3 0.7 pad_bitcast_fusion
  2.0 0.7 broadcast_select_fusion.lst_ref
  2.6 87.3 %gather_grad.1 = (bf16[2,8192,256]{2,1,0:T(8,128)(2,1)}, s32[2,384,128]{2,1,0:T(8,128)}, s32[2,256,128]{2,1,0:T(8,128)}, f32[256,128]{1,0:T(8,128)}, s32[256,128]{1,0:T(8,128)}, /*index=5*/s32[8,256]{1,0:T(8,128)}) custom-call(bf16[104,2048]{1,0:T(8,128)(2,1)} %tok_ref.1, bf16[104,2048]{1,0:T(8,128)(2,1)} %cot_ref.1, bf16[2048,256]{1,0:T(8,128)(2,1)} %w_in.1, ...), custom_call_target="tpu_custom_call" | custom-call | flops 15000000512 | bytes 20000000 | tf_op jit(solution)/shard_map/gather_grad/pallas_call | solution.py:618
  89.9 55.4 %sketch_reduce.1.table = f32[2816,128]{1,0:T(8,128)} custom-call(bf16[2,8192,256]{2,1,0:T(8,128)(2,1)} %get-tuple-element.14.ghl_ref, s32[2,384,128]{2,1,0:T(8,128)} %get-tuple-element.15.codes_ref, s32[2,256,128]{2,1,0:T(8,128)} %get-tuple-element.16.spots_ref), custom_call_target="tpu_custom_call" | custom-call | flops 24000000000 | bytes 10000000 | tf_op jit(solution)/shard_map/sketch_reduce/pallas_call | solution.py:664
  145.3 6.4 %finish.1 = (f32[2048,256]{1,0:T(8,128)}, f32[256,2048]{1,0:T(8,128)}, f32[512,5,128]{2,1,0:T(8,128)}, f32[512,5,128]{2,1,0:T(8,128)}) custom-call(f32[2816,128]{1,0:T(8,128)} %sketch_reduce.1.table, f32[256,128]{1,0:T(8,128)} %get-tuple-element.17.med, s32[256,128]{1,0:T(8,128)} %get-tuple-element.18.info, s32[8,256]{1,0:T(8,128)} %get-tuple-element.19.across, ...), custom_call_target="tpu_custom_call" | custom-call | flops 3000000000 | bytes 16000000 | tf_op jit(solution)/shard_map/finish/pallas_call | solution.py:748
  (1 shorter events, 0.0 us)

commit v2 on v1

--- a/solution.py
+++ b/solution.py
@@ -162,10 +162,10 @@
 
 
 def main_kernel(
-    tok_ref, cot_ref, win_ref, wout_ref, ord_ref, sgn_ref, lst_ref, mom_ref, err_ref,
+    tok_ref, cot_ref, win_ref, wout_ref, ord_ref, sgn_ref, lst_ref, cnt_ref, mom_ref, err_ref,
     ghl_ref, codes_ref, spots_ref, med_ref, info_ref, across_ref,
     own, land, buf, wi, wo, gin, gout, ordv, sgnv, meta, meta2, ghl,
-    momv, errv, medv, infov, acrossv, spots,
+    momv, errv, medv, infov, acrossv, spots, lstv,
     lsem, land_sem, ring_s, ring_r, sib_s, sib_r, w_s, w_r, list_s, list_r, meta_s, meta_r,
 ):
     rep, shard = lax.axis_index("rep"), lax.axis_index("shard")
@@ -194,7 +194,7 @@
     own_tok = pltpu.make_async_copy(tok_ref, own, lsem.at[0])
     own_cot = pltpu.make_async_copy(cot_ref, own, lsem.at[0])
     loads = [
-        pltpu.make_async_copy(lst_ref, meta.at[pl.ds(pl.multiple_of(CODE + 8 * rep, 8), 8)], lsem.at[1]),
+        pltpu.make_async_copy(lst_ref, lstv, lsem.at[1]),
         pltpu.make_async_copy(ord_ref, ordv, lsem.at[2]),
         pltpu.make_async_copy(sgn_ref, sgnv, lsem.at[3]),
     ]
@@ -231,6 +231,8 @@
     on_core(1, w_out_first.start, w_in_first.start)
 
     loads[0].wait()
+    listed = jnp.concatenate([lstv[...], jnp.full(lstv.shape, cnt_ref[0, 0], I32)], axis=1)
+    meta[pl.ds(pl.multiple_of(CODE + 8 * rep, 8), 8), :] = jnp.where(iota((8, 128), 0) == rep, listed, 0)
     list_row = meta.at[pl.ds(pl.multiple_of(CODE + 8 * rep, 8), 8)]
     peers = [(0, 1), (1, 0), (1, 1), (2, 0), (2, 1), (3, 0), (3, 1)]
     peers = [(n, dev(dy=d, to=other if flip else core)) for n, (d, flip) in enumerate(peers)]
@@ -311,10 +313,6 @@
     ]
     for copy in ready:
         copy.start()
-    arrive(2, 0)
-    on_core(0, w_out_first.wait_recv, own_wi.wait, own_wo.wait)
-    on_core(1, w_in_first.wait_recv)
-    arrive(2, 1)
     meta_first.wait_recv()
     on_core(1, meta_next.wait_recv)
     for k in (0, 1):
@@ -325,27 +323,44 @@
     ]
     for copy in ready[3:]:
         copy.start()
-    on_core(1, w_in_next.wait_recv, w_out_next.wait_recv)
-
-    def wait_sibling(slots):
-        for slot in slots:
-            for sub in (0, 1):
-                sibling(slot, sub).wait_recv()
+    arrive(2, 0)
+    on_core(0, w_out_first.wait_recv, own_wi.wait, own_wo.wait)
+    on_core(1, w_in_first.wait_recv, w_in_next.wait_recv, w_out_next.wait_recv)
+
+    def slots_of(hops, turn):
+        return (hops, (NZ - hops) % NZ) if turn == 0 else ((NZ - hops) % NZ, hops)
+
+    def wait_sibling(hops, turn):
+        for sub, slot in enumerate(slots_of(hops, turn)):
+            sibling(slot, sub).wait_recv()
+
+    out_first = pltpu.make_async_copy(ghl.at[:, pl.ds(0, 4096)], ghl_ref.at[:, pl.ds(0, 4096)], lsem.at[19])
+    out_last = pltpu.make_async_copy(ghl.at[:, pl.ds(4096, 4096)], ghl_ref.at[:, pl.ds(4096, 4096)], lsem.at[20])
+    ready += [out_first, out_last]
 
     def work(i, carry):
         @pl.when(i == 0)
         def _():
-            wait_sibling((0, 1, 7))
-
-        @pl.when(i == 3)
-        def _():
+            for hops, turn in ((0, 0), (1, 0), (1, 1), (2, 0)):
+                wait_sibling(hops, turn)
+
+        @pl.when(i == 2)
+        def _():
+            arrive(2, 1)
+
+        @pl.when(i == 4)
+        def _():
+            wait_sibling(2, 1)
             arrive(3, 0)
-            wait_sibling((2, 6))
 
         @pl.when(i == 5)
         def _():
+            wait_sibling(3, 0)
+
+        @pl.when(i == 6)
+        def _():
             arrive(3, 1)
-            wait_sibling((3, 5))
+            wait_sibling(3, 1)
 
         @pl.when(i == 7)
         def _():
@@ -353,32 +368,60 @@
             sibling(4, 0).start()
             ring(1, 3, 1).wait_recv()
             sibling(4, 1).start()
-            wait_sibling((4,))
-
-        slot = lax.rem(jnp.where(i % 2 == 1, (i + 1) // 2, NZ - i // 2), NZ)
-        rows = pl.ds(pl.multiple_of(slot * CHIP, 16), CHIP)
-
-        value, slope = gelu_pair(nn(buf[0, rows, :], wi[...]))
-        back = nt(buf[1, rows, :], wo[...])
+            wait_sibling(4, 0)
+
+        hops = (i + 1) // 2
+        slot_a = lax.rem(jnp.where(i % 2 == 1, hops, NZ - hops), NZ)
+        slot_b = lax.rem(NZ - slot_a, NZ)
+        rows_a = pl.ds(pl.multiple_of(slot_a * CHIP, 16), SUBS[0][1])
+        rows_b = pl.ds(pl.multiple_of(slot_b * CHIP + SUBS[1][0], 16), SUBS[1][1])
+
+        def rows(kind, at):
+            return jnp.concatenate([buf[kind, rows_a, at], buf[kind, rows_b, at]], axis=0)
+
+        everything = slice(None)
+        value, slope = gelu_pair(nn(rows(0, everything), wi[...]))
+        back = nt(rows(1, everything), wo[...])
         hidden = value.astype(BF16)
         grad = (back * slope).astype(BF16)
         for c in range(4):
             at = slice(c * 512, (c + 1) * 512)
-            gin[at, :] += tn(buf[0, rows, at], grad)
-            gout[:, at] += tn(hidden, buf[1, rows, at])
+            total = gin[at, :] + tn(rows(0, at), grad)
+
+            @pl.when(i < 7)
+            def _(at=at, total=total):
+                gin[at, :] = total
+
+            @pl.when(i == 7)
+            def _(c=c, total=total):
+                for k in range(2):
+                    for h in range(2):
+                        part = total[:, k * COLS + h * 128 : k * COLS + (h + 1) * 128]
+                        ghl[k, h * 2048 + c * 512 : h * 2048 + (c + 1) * 512, :] = split2(part)
+
+        @pl.when(i == 7)
+        def _():
+            out_first.start()
+
+        for c in range(4):
+            at = slice(c * 512, (c + 1) * 512)
+            total = gout[:, at] + tn(hidden, rows(1, at))
+
+            @pl.when(i < 7)
+            def _(at=at, total=total):
+                gout[:, at] = total
+
+            @pl.when(i == 7)
+            def _(c=c, total=total):
+                for k in range(2):
+                    for q in range(4 * c, 4 * c + 4):
+                        part = total[k * COLS : (k + 1) * COLS, (q - 4 * c) * 128 : (q - 4 * c + 1) * 128]
+                        ghl[k, 4096 + q * 256 : 4352 + q * 256, :] = split2(part)
+
         return carry
 
     lax.fori_loop(0, NZ, work, 0)
-
-    for k in (1, 0):
-        for h in range(2):
-            at = slice(k * COLS + h * 128, k * COLS + (h + 1) * 128)
-            ghl[k, h * 2048 : (h + 1) * 2048, :] = split2(gin[:, at])
-        for q in range(16):
-            part = gout[k * COLS : (k + 1) * COLS, q * 128 : (q + 1) * 128]
-            ghl[k, 4096 + q * 256 : 4352 + q * 256, :] = split2(part)
-        ready.append(pltpu.make_async_copy(ghl.at[k], ghl_ref.at[k], lsem.at[19 + k]))
-        ready[-1].start()
+    out_last.start()
 
     for copy in list_copies + [w_in_first, w_out_first, meta_first]:
         copy.wait_send()
@@ -433,64 +476,69 @@
         load.start()
     barrier = pltpu.get_barrier_semaphore()
     partners = [dev(dx=d, to=c) for d in (1, -1, 2) for c in (0, 1)]
-    partners += [dev(dy=d, to=c) for d in (1, 2, 3) for c in (0, 1)] + [dev(to=other)]
+    partners += [dev(dy=d) for d in (1, 2, 3)] + [dev(to=other)]
     for partner in partners:
         pl.semaphore_signal(barrier, inc=1, device_id=partner, device_id_type=MESH)
     pl.semaphore_wait(barrier, len(partners))
-    peers = [(0, 1), (1, 0), (1, 1), (2, 0), (2, 1), (3, 0), (3, 1)]
-    peers = [(n, dev(dy=d, to=other if flip else core)) for n, (d, flip) in enumerate(peers)]
     loads[0].wait()
     loads[1].wait()
 
-    def one_hot(code, parts):
+    def spread(code):
+        code = jnp.broadcast_to(code, (16, 128))
+        bucket = (code >> 1).astype(F32)
+        return jnp.where((code & 1) == 1, 1.0, -1.0).astype(BF16), [(bucket - 256.0 * h).astype(BF16) for h in (0, 1)]
+
+    def one_hot(spread_code, quarter):
+        sign, spot = spread_code[0], spread_code[1][quarter // 2]
         ramp = iota((256, 128), 0).astype(F32).astype(BF16)
-        code = jnp.broadcast_to(code, (16, 128))
-        sign = jnp.where((code & 1) == 1, 1.0, -1.0).astype(BF16)
-        bucket = (code >> 1).astype(F32)
-        rows = []
-        for part in parts:
-            spot = (bucket - 256.0 * part).astype(BF16)
-            for g in range(16):
-                rows.append(jnp.where(spot == ramp[g * 16 : (g + 1) * 16], sign, jnp.zeros_like(sign)))
-        return jnp.concatenate(rows, axis=0)
-
-    def sketch(k, left, right, listed):
+        first = 8 * (quarter % 2)
+        hits = [spot == ramp[g * 16 : (g + 1) * 16] for g in range(first, first + 8)]
+        return jnp.concatenate([jnp.where(hit, sign, jnp.zeros_like(sign)) for hit in hits], axis=0)
+
+    def sketch(k, work):
         step = 8
-        parts = left[1]
+        count = len(work[0])
 
         def run(*sums):
             def chunk(t, carry):
                 tiles = [ghl[k, pl.ds(pl.multiple_of((t * step + i) * 256, 256), 256), :] for i in range(step)]
-                found = [codes[k, pl.ds(pl.multiple_of(j * 64 + t * 2 * step, 16), 2 * step), :] for j, _ in (left, right)]
+                used = sorted({j for part in work[0] + work[1] for j in part[:1] if j is not None})
+                found = {j: codes[k, pl.ds(pl.multiple_of(j * 64 + t * 2 * step, 16), 2 * step), :] for j in used}
                 for unit in (0, 1):
                     pltpu.matmul_push_rhs(tiles[0], 0, unit)
                 for i in range(step):
                     if i + 1 < step:
                         for unit in (0, 1):
                             pltpu.matmul_push_rhs(tiles[i + 1], (i + 1) % 2, unit)
-                    for unit in (0, 1):
-                        code = found[unit][2 * i : 2 * i + 2, :]
-                        hot = [one_hot(code[n : n + 1, :], (left, right)[unit][1]) for n in (0, 1)]
-                        pltpu.matmul_acc_lhs(sums[unit], jnp.concatenate(hot, axis=1), load_staged_rhs=i % 2)
-                        if listed:
-                            spot = spots[k, unit * 128 : (unit + 1) * 128, :] - (t * step + i) * 256
-                            lane = iota((128, 128), 1)
-                            hot = [jnp.where(spot == lane + 128 * n, 1.0, 0.0).astype(BF16) for n in (0, 1)]
-                            pltpu.matmul_acc_lhs(sums[2 + unit], jnp.concatenate(hot, axis=1))
+                    rows = {j: [spread(found[j][2 * i + n : 2 * i + n + 1, :]) for n in (0, 1)] for j in used}
+                    for c in range(count):
+                        for unit in (0, 1):
+                            j, q = work[unit][c]
+                            if j is None:
+                                spot = spots[k, q * 128 : (q + 1) * 128, :] - (t * step + i) * 256
+                                lane = iota((128, 128), 1)
+                                hot = [jnp.where(spot == lane + 128 * n, 1.0, 0.0).astype(BF16) for n in (0, 1)]
+                            else:
+                                hot = [one_hot(rows[j][n], q) for n in (0, 1)]
+                            pltpu.matmul_acc_lhs(
+                                sums[2 * c + unit],
+                                jnp.concatenate(hot, axis=1),
+                                load_staged_rhs=i % 2 if c == 0 else None,
+                            )
                 return carry
 
             lax.fori_loop(0, 32 // step, chunk, 0)
-            for unit in (0, 1):
-                j, part = (left, right)[unit]
-                total = pltpu.matmul_pop(sums[unit])
-                start = LIVE + j * COUNT + part[0] * 256
-                outb[k, start : start + len(part) * 256, :] = (total[:, :128] + total[:, 128:]).astype(BF16)
-                if listed:
-                    total = pltpu.matmul_pop(sums[2 + unit])
-                    outb[k, unit * 128 : (unit + 1) * 128, :] = (total[:, :128] + total[:, 128:]).astype(BF16)
-
-        rows = [256 * len(parts)] + ([128] if listed else [])
-        pl.run_scoped(run, *[pltpu.ACC(mxu_id=unit)((n, 256), F32) for n in rows for unit in (0, 1)])
+            for c in range(count):
+                for unit in (0, 1):
+                    j, q = work[unit][c]
+                    total = pltpu.matmul_pop(sums[2 * c + unit])
+                    start = q * 128 + (0 if j is None else LIVE + j * COUNT)
+                    outb[k, start : start + 128, :] = (total[:, :128] + total[:, 128:]).astype(BF16)
+
+        pl.run_scoped(run, *[pltpu.ACC(mxu_id=unit)((128, 256), F32) for c in range(count) for unit in (0, 1)])
+
+    def whole(j):
+        return [(j, q) for q in range(4)]
 
     def half_of(p):
         return PIECES[p][0] // 2, PIECES[p][1] // 2
@@ -544,9 +592,9 @@
         for d in (1, 2, 3):
             y_copy(p, d).start()
 
-    def a_copy(p, n, peer):
+    def a_copy(p, d):
         at = tot.at[my_quarter(p)]
-        return remote(at, at, a_s.at[p, n], a_r.at[p, n], peer)
+        return remote(at, at, a_s.at[p, d - 1], a_r.at[p, d - 1], dev(dy=d))
 
     def a_start(p):
         start, rows = quarter_of(p)
@@ -555,64 +603,54 @@
             y_copy(p, d).wait_recv()
             total = total + recvy[d - 1, start : start + rows, :].astype(F32)
         tot[my_quarter(p), :] = total
-        for n, peer in peers:
-            a_copy(p, n, peer).start()
-
-    def step(t, carry):
-        k = jnp.where(t < 3, 1, 0)
-        part = lax.rem(t, 3)
-
-        @pl.when(part == 0)
-        def _():
-            @pl.when(t == 0)
-            def _():
-                loads[2].wait()
-
-            @pl.when(t == 3)
-            def _():
-                loads[3].wait()
-
-            sketch(k, (0, (0, 1)), (1, (0, 1)), True)
-
-        @pl.when(part == 1)
-        def _():
-            sketch(k, (2, (0, 1)), (3, (0, 1)), False)
-
-        @pl.when(part == 2)
-        def _():
-            sketch(k, (4, (0,)), (4, (1,)), False)
-
-        for when, action, p in (
-            (0, x_far_start, 0), (1, x_far_start, 1), (2, x_far_start, 2),
-            (3, x_near_start, 0), (4, x_near_start, 1), (4, y_start, 0), (5, x_near_start, 2), (5, a_start, 0),
-            (5, y_start, 1),
-        ):
-
-            @pl.when(t == when)
-            def _(action=action, p=p):
-                action(p)
-
-        return carry
-
-    lax.fori_loop(0, 6, step, 0)
+        for d in (1, 2, 3):
+            a_copy(p, d).start()
+
+    def e_copy(p):
+        rows = PIECES[p][1] // 2
+        at = tot.at[pl.ds(pl.multiple_of(PIECES[p][0] + core * rows, 16), rows)]
+        return remote(at, at, a_s.at[p, 3], a_r.at[p, 3], dev(to=other))
+
+    def e_start(p):
+        for d in (1, 2, 3):
+            a_copy(p, d).wait_recv()
+        e_copy(p).start()
+
+    loads[2].wait()
+    sketch(1, (whole(0) + whole(2), whole(1) + whole(3)))
+    x_far_start(1)
+    sketch(1, ([(4, 0), (4, 1), (None, 0)], [(4, 2), (4, 3), (None, 1)]))
+    x_far_start(0)
+    x_far_start(2)
+    loads[3].wait()
+    sketch(0, (whole(0) + [(None, 0)], whole(1) + [(None, 1)]))
+    x_near_start(0)
+    sketch(0, (whole(2), whole(3)))
+    x_near_start(1)
+    y_start(0)
+    sketch(0, ([(4, 0), (4, 1)], [(4, 2), (4, 3)]))
+    x_near_start(2)
+    a_start(0)
+    y_start(1)
     y_start(2)
     a_start(1)
     a_start(2)
     for p in range(3):
-        for n, peer in peers:
-            a_copy(p, n, peer).wait_recv()
+        e_start(p)
+    for p in range(3):
+        e_copy(p).wait_recv()
     result = pltpu.make_async_copy(tot, table_ref, lsem.at[4])
     result.start()
 
     for p in range(3):
-        for copy in x_far[p] + [y_copy(p, d) for d in (1, 2, 3)] + [a_copy(p, n, peer) for n, peer in peers]:
+        for copy in x_far[p] + [y_copy(p, d) for d in (1, 2, 3)] + [a_copy(p, d) for d in (1, 2, 3)] + [e_copy(p)]:
             copy.wait_send()
     on_core(0, *[copy.wait_send for copy in x_home])
     on_core(1, *[c.wait_send for p in range(3) for c in x_near[p]])
     result.wait()
 
 
-def run_main(tokens, cotangent, w_in, w_out, order, signs, lists, mom, err):
+def run_main(*args):
     anywhere = pl.BlockSpec(memory_space=pl.ANY)
     dma = pltpu.SemaphoreType.DMA
     return pl.pallas_call(
@@ -625,7 +663,7 @@
             jax.ShapeDtypeStruct((LIVE, 128), I32),
             jax.ShapeDtypeStruct((8, LIVE), I32),
         ),
-        in_specs=[anywhere] * 9,
+        in_specs=[anywhere] * 7 + [pl.BlockSpec(memory_space=pltpu.SMEM)] + [anywhere] * 2,
         out_specs=(anywhere,) * 6,
         scratch_shapes=[
             pltpu.VMEM((TOK, DW), BF16),
@@ -646,6 +684,7 @@
             pltpu.VMEM((LIVE, 128), I32),
             pltpu.VMEM((8, LIVE), I32),
             pltpu.VMEM((2, LIVE, 128), I32),
+            pltpu.VMEM((1, 64), I32),
             dma((23,)), dma((2,)),
             dma((2, 4, 2)), dma((2, 4, 2)), dma((NZ, 2)), dma((NZ, 2)), dma((4,)), dma((4,)),
             dma((7,)), dma((7,)), dma((2,)), dma((2,)),
@@ -655,7 +694,7 @@
         ),
         cost_estimate=pl.CostEstimate(flops=15_000_000_000, bytes_accessed=20_000_000, transcendentals=2_000_000),
         name="gather_grad",
-    )(tokens, cotangent, w_in, w_out, order, signs, lists, mom, err)
+    )(*args)
 
 
 def run_sketch(ghl, codes, spots):
@@ -675,7 +714,7 @@
             pltpu.VMEM((TAB // 2, 128), BF16),
             pltpu.VMEM((3, TAB // 8, 128), BF16),
             pltpu.VMEM((TAB, 128), F32),
-            dma((5,)), dma((2, 3, 2)), dma((4, 3)), dma((3, 3)), dma((3, 3)), dma((3, 7)), dma((3, 7)),
+            dma((5,)), dma((2, 3, 2)), dma((4, 3)), dma((3, 3)), dma((3, 3)), dma((3, 4)), dma((3, 4)),
         ],
         compiler_params=pltpu.CompilerParams(
             collective_id=1, has_side_effects=True, vmem_limit_bytes=62 * 1024 * 1024
@@ -769,12 +808,9 @@
 def per_device(
     tokens, cotangent, w_in, w_out, momentum, error, block_order, signs, heavy_blocks, heavy_count
 ):
-    listed = jnp.concatenate([heavy_blocks, jnp.broadcast_to(heavy_count, heavy_blocks.shape)], axis=1)
-    here = lax.broadcasted_iota(I32, (8, 128), 0) == lax.axis_index("rep")
-    lists = jnp.where(here, listed, 0)
     mom, err = by_bucket(momentum), by_bucket(error)
     ghl, codes, spots, med, info, across = run_main(
-        tokens, cotangent, w_in, w_out, block_order, signs, lists, mom, err
+        tokens, cotangent, w_in, w_out, block_order, signs, heavy_blocks, heavy_count, mom, err
     )
     table = run_sketch(ghl, codes, spots)
     win_new, wout_new, mom_new, err_new = run_finish(table, med, info, across, mom, err, w_in, w_out)

time: 152 us -> 149 us (0.980)
  Pallas kernels: 149 us -> 147 us
    pallas_call x1, Pallas kernels: 55.4 us -> 49.7 us  [run_sketch(): pl.pallas_call(sketch_kernel, out_shape=jax.ShapeDtypeStruct((TAB, 128),...]
    pallas_call x1, Pallas kernels: 87.3 us -> 90.9 us  [run_main(): pl.pallas_call(main_kernel, out_shape=(jax.ShapeDtypeStruct((2, NB, 256),...]
where the time goes in v2:
time: 149 us
  Pallas kernels  147 us (99%)
    pallas_call x1, Pallas kernels, run_main(): pl.pallas_call(main_kernel, out_shape=(jax.ShapeDtypeStruct((2, NB, 256),...  90.9 us
    pallas_call x1, Pallas kernels, run_sketch(): pl.pallas_call(sketch_kernel, out_shape=jax.ShapeDtypeStruct((TAB, 128),...  49.7 us
    pallas_call x1, Pallas kernels, run_finish(): pl.pallas_call(finish_kernel, out_shape=(jax.ShapeDtypeStruct(w_in.shape,...  6.42 us

profile of v2, /device:TPU:1, one launch (start us, length us, event | category | flops | bytes accessed | tf_op | source)
XLA Modules:
  0.0 148.5 jit_solution(9925324677576046474)
XLA Ops:
  1.3 90.9 %gather_grad.1 = (bf16[2,8192,256]{2,1,0:T(8,128)(2,1)}, s32[2,384,128]{2,1,0:T(8,128)}, s32[2,256,128]{2,1,0:T(8,128)}, f32[256,128]{1,0:T(8,128)}, s32[256,128]{1,0:T(8,128)}, /*index=5*/s32[8,256]{1,0:T(8,128)}) custom-call(bf16[104,2048]{1,0:T(8,128)(2,1)} %tok_ref.1, bf16[104,2048]{1,0:T(8,128)(2,1)} %cot_ref.1, bf16[2048,256]{1,0:T(8,128)(2,1)} %w_in.1, ...), custom_call_target="tpu_custom_call" | custom-call | flops 15000000512 | bytes 20000000 | tf_op jit(solution)/shard_map/gather_grad/pallas_call | solution.py:656
  92.2 49.7 %sketch_reduce.1.table = f32[2816,128]{1,0:T(8,128)} custom-call(bf16[2,8192,256]{2,1,0:T(8,128)(2,1)} %get-tuple-element.14.ghl_ref, s32[2,384,128]{2,1,0:T(8,128)} %get-tuple-element.15.codes_ref, s32[2,256,128]{2,1,0:T(8,128)} %get-tuple-element.16.spots_ref), custom_call_target="tpu_custom_call" | custom-call | flops 24000000000 | bytes 10000000 | tf_op jit(solution)/shard_map/sketch_reduce/pallas_call | solution.py:703
  141.9 6.4 %finish.1 = (f32[2048,256]{1,0:T(8,128)}, f32[256,2048]{1,0:T(8,128)}, f32[512,5,128]{2,1,0:T(8,128)}, f32[512,5,128]{2,1,0:T(8,128)}) custom-call(f32[2816,128]{1,0:T(8,128)} %sketch_reduce.1.table, f32[256,128]{1,0:T(8,128)} %get-tuple-element.17.med, s32[256,128]{1,0:T(8,128)} %get-tuple-element.18.info, s32[8,256]{1,0:T(8,128)} %get-tuple-element.19.across, ...), custom_call_target="tpu_custom_call" | custom-call | flops 3000000000 | bytes 16000000 | tf_op jit(solution)/shard_map/finish/pallas_call | solution.py:787

commit v3 on v2

--- a/solution.py
+++ b/solution.py
@@ -22,8 +22,9 @@
 COUNT = 512
 ROWS = 5
 LIVE = 256
-TAB = LIVE + ROWS * COUNT
-PIECES = ((0, 1280), (1280, 1024), (2304, 512))
+LISTED = ROWS * COUNT
+TAB = LISTED + LIVE
+PIECES = ((0, 1024), (1024, 1024), (2048, 768))
 CODE = ROWS * 64
 META = CODE + 64
 
@@ -248,23 +249,27 @@
         first, second = jnp.where(core == 0, mine, theirs), jnp.where(core == 0, theirs, mine)
         buf[core, 0:CHIP, at] = jnp.concatenate([first, second], axis=0).astype(BF16)
 
-    def slot_of(way, hops):
-        return hops if way == 0 else (NZ - hops) % NZ
-
-    def rows_of(slot, sub):
-        return pl.ds(slot * CHIP + SUBS[sub][0], SUBS[sub][1])
+    def turn_of(way, sub):
+        return sub if way == 0 else 1 - sub
+
+    def unit_of(hops, turn):
+        return 0 if hops == 0 else 2 * hops - 1 + turn
+
+    def rows_of(unit, sub):
+        return pl.ds(unit * CHIP + SUBS[sub][0], SUBS[sub][1])
 
     def ring(way, hops, sub):
+        turn = turn_of(way, sub)
         return remote(
-            buf.at[core, rows_of(slot_of(way, hops), sub)],
-            buf.at[core, rows_of(slot_of(way, hops + 1), sub)],
+            buf.at[core, rows_of(unit_of(hops, turn), sub)],
+            buf.at[core, rows_of(unit_of(hops + 1, turn), sub)],
             ring_s.at[way, hops, sub], ring_r.at[way, hops, sub],
             dev(dz=1 if way == 0 else -1),
         )
 
-    def sibling(slot, sub):
-        at = buf.at[core, rows_of(slot, sub)]
-        return remote(at, at, sib_s.at[slot, sub], sib_r.at[slot, sub], dev(to=other))
+    def sibling(unit, sub):
+        at = buf.at[core, rows_of(unit, sub)]
+        return remote(at, at, sib_s.at[unit, sub], sib_r.at[unit, sub], dev(to=other))
 
     for turn in (0, 1):
         ring(0, 0, turn).start()
@@ -280,7 +285,7 @@
             ring(way, hops - 1, sub).wait_recv()
             if hops < 3 or (hops == 3 and turn == 0):
                 ring(way, hops, sub).start()
-            sibling(slot_of(way, hops), sub).start()
+            sibling(unit_of(hops, turn), sub).start()
 
     loads[1].wait()
     loads[2].wait()
@@ -327,100 +332,72 @@
     on_core(0, w_out_first.wait_recv, own_wi.wait, own_wo.wait)
     on_core(1, w_in_first.wait_recv, w_in_next.wait_recv, w_out_next.wait_recv)
 
-    def slots_of(hops, turn):
-        return (hops, (NZ - hops) % NZ) if turn == 0 else ((NZ - hops) % NZ, hops)
-
-    def wait_sibling(hops, turn):
-        for sub, slot in enumerate(slots_of(hops, turn)):
-            sibling(slot, sub).wait_recv()
+    def wait_sibling(*units):
+        for unit in units:
+            for sub in (0, 1):
+                sibling(unit, sub).wait_recv()
 
     out_first = pltpu.make_async_copy(ghl.at[:, pl.ds(0, 4096)], ghl_ref.at[:, pl.ds(0, 4096)], lsem.at[19])
     out_last = pltpu.make_async_copy(ghl.at[:, pl.ds(4096, 4096)], ghl_ref.at[:, pl.ds(4096, 4096)], lsem.at[20])
     ready += [out_first, out_last]
 
-    def work(i, carry):
-        @pl.when(i == 0)
-        def _():
-            for hops, turn in ((0, 0), (1, 0), (1, 1), (2, 0)):
-                wait_sibling(hops, turn)
-
-        @pl.when(i == 2)
-        def _():
-            arrive(2, 1)
-
-        @pl.when(i == 4)
-        def _():
-            wait_sibling(2, 1)
-            arrive(3, 0)
-
-        @pl.when(i == 5)
-        def _():
-            wait_sibling(3, 0)
-
-        @pl.when(i == 6)
-        def _():
-            arrive(3, 1)
-            wait_sibling(3, 1)
-
-        @pl.when(i == 7)
-        def _():
-            ring(0, 3, 0).wait_recv()
-            sibling(4, 0).start()
-            ring(1, 3, 1).wait_recv()
-            sibling(4, 1).start()
-            wait_sibling(4, 0)
-
-        hops = (i + 1) // 2
-        slot_a = lax.rem(jnp.where(i % 2 == 1, hops, NZ - hops), NZ)
-        slot_b = lax.rem(NZ - slot_a, NZ)
-        rows_a = pl.ds(pl.multiple_of(slot_a * CHIP, 16), SUBS[0][1])
-        rows_b = pl.ds(pl.multiple_of(slot_b * CHIP + SUBS[1][0], 16), SUBS[1][1])
-
-        def rows(kind, at):
-            return jnp.concatenate([buf[kind, rows_a, at], buf[kind, rows_b, at]], axis=0)
-
-        everything = slice(None)
-        value, slope = gelu_pair(nn(rows(0, everything), wi[...]))
-        back = nt(rows(1, everything), wo[...])
+    def work(start, count, last=False):
+        rows = pl.ds(start, count)
+        value, slope = gelu_pair(nn(buf[0, rows, :], wi[...]))
+        back = nt(buf[1, rows, :], wo[...])
         hidden = value.astype(BF16)
         grad = (back * slope).astype(BF16)
         for c in range(4):
             at = slice(c * 512, (c + 1) * 512)
-            total = gin[at, :] + tn(rows(0, at), grad)
-
-            @pl.when(i < 7)
-            def _(at=at, total=total):
+            total = gin[at, :] + tn(buf[0, rows, at], grad)
+            if not last:
                 gin[at, :] = total
-
-            @pl.when(i == 7)
-            def _(c=c, total=total):
-                for k in range(2):
-                    for h in range(2):
-                        part = total[:, k * COLS + h * 128 : k * COLS + (h + 1) * 128]
-                        ghl[k, h * 2048 + c * 512 : h * 2048 + (c + 1) * 512, :] = split2(part)
-
-        @pl.when(i == 7)
-        def _():
+                continue
+            for k in range(2):
+                for h in range(2):
+                    part = total[:, k * COLS + h * 128 : k * COLS + (h + 1) * 128]
+                    ghl[k, h * 2048 + c * 512 : h * 2048 + (c + 1) * 512, :] = split2(part)
+        if last:
             out_first.start()
-
         for c in range(4):
             at = slice(c * 512, (c + 1) * 512)
-            total = gout[:, at] + tn(hidden, rows(1, at))
-
-            @pl.when(i < 7)
-            def _(at=at, total=total):
+            total = gout[:, at] + tn(hidden, buf[1, rows, at])
+            if not last:
                 gout[:, at] = total
-
-            @pl.when(i == 7)
-            def _(c=c, total=total):
-                for k in range(2):
-                    for q in range(4 * c, 4 * c + 4):
-                        part = total[k * COLS : (k + 1) * COLS, (q - 4 * c) * 128 : (q - 4 * c + 1) * 128]
-                        ghl[k, 4096 + q * 256 : 4352 + q * 256, :] = split2(part)
-
+                continue
+            for k in range(2):
+                for q in range(4 * c, 4 * c + 4):
+                    part = total[k * COLS : (k + 1) * COLS, (q - 4 * c) * 128 : (q - 4 * c + 1) * 128]
+                    ghl[k, 4096 + q * 256 : 4352 + q * 256, :] = split2(part)
+
+    def work_pair(i, carry):
+        @pl.when(i == 0)
+        def _():
+            wait_sibling(0, 1)
+
+        @pl.when(i == 1)
+        def _():
+            wait_sibling(2, 3)
+
+        @pl.when(i == 2)
+        def _():
+            arrive(2, 1)
+            arrive(3, 0)
+            wait_sibling(4, 5)
+
+        work(pl.multiple_of(i * (2 * CHIP), 16), 2 * CHIP)
         return carry
 
-    lax.fori_loop(0, NZ, work, 0)
+    lax.fori_loop(0, 3, work_pair, 0)
+    arrive(3, 1)
+    wait_sibling(6)
+    work(6 * CHIP, CHIP)
+    ring(0, 3, 0).wait_recv()
+    sibling(7, 0).start()
+    ring(1, 3, 1).wait_recv()
+    sibling(7, 1).start()
+    wait_sibling(7)
+    work(7 * CHIP, CHIP, last=True)
     out_last.start()
 
     for copy in list_copies + [w_in_first, w_out_first, meta_first]:
@@ -430,9 +407,9 @@
             for sub in (0, 1):
                 if hops < 3 or sub == way:
                     ring(way, hops, sub).wait_send()
-    for slot in range(NZ):
+    for unit in range(NZ):
         for sub in (0, 1):
-            sibling(slot, sub).wait_send()
+            sibling(unit, sub).wait_send()
     on_core(0, w_in_next.wait_send)
     on_core(1, w_out_next.wait_send, meta_next.wait_send)
     for copy in ready:
@@ -496,30 +473,39 @@
         return jnp.concatenate([jnp.where(hit, sign, jnp.zeros_like(sign)) for hit in hits], axis=0)
 
     def sketch(k, work):
-        step = 8
-        count = len(work[0])
+        step = 4
+        per = NB // 512
+        used = sorted({j for j, _ in work if j is not None})
 
         def run(*sums):
             def chunk(t, carry):
-                tiles = [ghl[k, pl.ds(pl.multiple_of((t * step + i) * 256, 256), 256), :] for i in range(step)]
-                used = sorted({j for part in work[0] + work[1] for j in part[:1] if j is not None})
-                found = {j: codes[k, pl.ds(pl.multiple_of(j * 64 + t * 2 * step, 16), 2 * step), :] for j in used}
+                first = [unit * per + t * step for unit in (0, 1)]
+
+                def tile(unit, i):
+                    return ghl[k, pl.ds(pl.multiple_of((first[unit] + i) * 256, 256), 256), :]
+
+                found = [
+                    {j: codes[k, pl.ds(pl.multiple_of(j * 64 + 2 * first[unit], 8), 2 * step), :] for j in used}
+                    for unit in (0, 1)
+                ]
                 for unit in (0, 1):
-                    pltpu.matmul_push_rhs(tiles[0], 0, unit)
+                    pltpu.matmul_push_rhs(tile(unit, 0), 0, unit)
                 for i in range(step):
                     if i + 1 < step:
                         for unit in (0, 1):
-                            pltpu.matmul_push_rhs(tiles[i + 1], (i + 1) % 2, unit)
-                    rows = {j: [spread(found[j][2 * i + n : 2 * i + n + 1, :]) for n in (0, 1)] for j in used}
-                    for c in range(count):
+                            pltpu.matmul_push_rhs(tile(unit, i + 1), (i + 1) % 2, unit)
+                    rows = [
+                        {j: [spread(found[unit][j][2 * i + n : 2 * i + n + 1, :]) for n in (0, 1)] for j in used}
+                        for unit in (0, 1)
+                    ]
+                    for c, (j, q) in enumerate(work):
                         for unit in (0, 1):
-                            j, q = work[unit][c]
                             if j is None:
-                                spot = spots[k, q * 128 : (q + 1) * 128, :] - (t * step + i) * 256
+                                spot = spots[k, q * 128 : (q + 1) * 128, :] - (first[unit] + i) * 256
                                 lane = iota((128, 128), 1)
                                 hot = [jnp.where(spot == lane + 128 * n, 1.0, 0.0).astype(BF16) for n in (0, 1)]
                             else:
-                                hot = [one_hot(rows[j][n], q) for n in (0, 1)]
+                                hot = [one_hot(rows[unit][j][n], q) for n in (0, 1)]
                             pltpu.matmul_acc_lhs(
                                 sums[2 * c + unit],
                                 jnp.concatenate(hot, axis=1),
@@ -527,18 +513,16 @@
                             )
                 return carry
 
-            lax.fori_loop(0, 32 // step, chunk, 0)
-            for c in range(count):
-                for unit in (0, 1):
-                    j, q = work[unit][c]
-                    total = pltpu.matmul_pop(sums[2 * c + unit])
-                    start = q * 128 + (0 if j is None else LIVE + j * COUNT)
-                    outb[k, start : start + 128, :] = (total[:, :128] + total[:, 128:]).astype(BF16)
-
-        pl.run_scoped(run, *[pltpu.ACC(mxu_id=unit)((128, 256), F32) for c in range(count) for unit in (0, 1)])
-
-    def whole(j):
-        return [(j, q) for q in range(4)]
+            lax.fori_loop(0, per // step, chunk, 0)
+            for c, (j, q) in enumerate(work):
+                total = pltpu.matmul_pop(sums[2 * c]) + pltpu.matmul_pop(sums[2 * c + 1])
+                start = q * 128 + (LISTED if j is None else j * COUNT)
+                outb[k, start : start + 128, :] = (total[:, :128] + total[:, 128:]).astype(BF16)
+
+        pl.run_scoped(run, *[pltpu.ACC(mxu_id=unit)((128, 256), F32) for _ in work for unit in (0, 1)])
+
+    def whole(*rows):
+        return [(j, q) for j in rows for q in range(4)]
 
     def half_of(p):
         return PIECES[p][0] // 2, PIECES[p][1] // 2
@@ -616,19 +600,18 @@
             a_copy(p, d).wait_recv()
         e_copy(p).start()
 
+    passes = (whole(0, 1), whole(2, 3), whole(4) + [(None, 0), (None, 1)])
     loads[2].wait()
-    sketch(1, (whole(0) + whole(2), whole(1) + whole(3)))
-    x_far_start(1)
-    sketch(1, ([(4, 0), (4, 1), (None, 0)], [(4, 2), (4, 3), (None, 1)]))
-    x_far_start(0)
-    x_far_start(2)
+    for p in range(3):
+        sketch(1, passes[p])
+        x_far_start(p)
     loads[3].wait()
-    sketch(0, (whole(0) + [(None, 0)], whole(1) + [(None, 1)]))
+    sketch(0, passes[0])
     x_near_start(0)
-    sketch(0, (whole(2), whole(3)))
+    sketch(0, passes[1])
     x_near_start(1)
     y_start(0)
-    sketch(0, ([(4, 0), (4, 1)], [(4, 2), (4, 3)]))
+    sketch(0, passes[2])
     x_near_start(2)
     a_start(0)
     y_start(1)
@@ -744,7 +727,7 @@
     for load in loads[:4]:
         load.wait()
     codes = infov[...]
-    update = medv[...] + LEARN * tabv[:LIVE, :]
+    update = medv[...] + LEARN * tabv[LISTED:, :]
     kept = split2(jnp.where(codes[:, ROWS : ROWS + 1] == 1, update, 0.0))
     places = acrossv[0:1, :]
 
@@ -770,7 +753,7 @@
     for j in range(ROWS):
         loads[6 + 2 * j].wait()
         loads[7 + 2 * j].wait()
-        fresh = DECAY * momv[j] + tabv[LIVE + j * COUNT : LIVE + (j + 1) * COUNT, :]
+        fresh = DECAY * momv[j] + tabv[j * COUNT : (j + 1) * COUNT, :]
         momn[j] = fresh
         store(momn.at[j], mom_new.at[:, j, :])
         gone = tn(signed_hit(codes[:, j : j + 1]), kept)

time: 149 us -> 140 us (0.940)
  Pallas kernels: 147 us -> 139 us
    pallas_call x1, Pallas kernels: 90.9 us -> 84.1 us  [run_main(): pl.pallas_call(main_kernel, out_shape=(jax.ShapeDtypeStruct((2, NB, 256),...]
where the time goes in v3:
time: 140 us
  Pallas kernels  139 us (99%)
  between operations  1.48 us (1%)
    pallas_call x1, Pallas kernels, run_main(): pl.pallas_call(main_kernel, out_shape=(jax.ShapeDtypeStruct((2, NB, 256),...  84.1 us
    pallas_call x1, Pallas kernels, run_sketch(): pl.pallas_call(sketch_kernel, out_shape=jax.ShapeDtypeStruct((TAB, 128),...  48.4 us
    pallas_call x1, Pallas kernels, run_finish(): pl.pallas_call(finish_kernel, out_shape=(jax.ShapeDtypeStruct(w_in.shape,...  6.42 us

profile of v3, /device:TPU:1, one launch (start us, length us, event | category | flops | bytes accessed | tf_op | source)
XLA Modules:
  0.0 140.4 jit_solution(8221527864129539227)
XLA Ops:
  1.3 84.1 %gather_grad.1 = (bf16[2,8192,256]{2,1,0:T(8,128)(2,1)}, s32[2,384,128]{2,1,0:T(8,128)}, s32[2,256,128]{2,1,0:T(8,128)}, f32[256,128]{1,0:T(8,128)}, s32[256,128]{1,0:T(8,128)}, /*index=5*/s32[8,256]{1,0:T(8,128)}) custom-call(bf16[104,2048]{1,0:T(8,128)(2,1)} %tok_ref.1, bf16[104,2048]{1,0:T(8,128)(2,1)} %cot_ref.1, bf16[2048,256]{1,0:T(8,128)(2,1)} %w_in.1, ...), custom_call_target="tpu_custom_call" | custom-call | flops 15000000512 | bytes 20000000 | tf_op jit(solution)/shard_map/gather_grad/pallas_call | solution.py:639
  85.4 48.4 %sketch_reduce.1.table = f32[2816,128]{1,0:T(8,128)} custom-call(bf16[2,8192,256]{2,1,0:T(8,128)(2,1)} %get-tuple-element.14.ghl_ref, s32[2,384,128]{2,1,0:T(8,128)} %get-tuple-element.15.codes_ref, s32[2,256,128]{2,1,0:T(8,128)} %get-tuple-element.16.spots_ref), custom_call_target="tpu_custom_call" | custom-call | flops 24000000000 | bytes 10000000 | tf_op jit(solution)/shard_map/sketch_reduce/pallas_call | solution.py:686
  133.8 6.4 %finish.1 = (f32[2048,256]{1,0:T(8,128)}, f32[256,2048]{1,0:T(8,128)}, f32[512,5,128]{2,1,0:T(8,128)}, f32[512,5,128]{2,1,0:T(8,128)}) custom-call(f32[2816,128]{1,0:T(8,128)} %sketch_reduce.1.table, f32[256,128]{1,0:T(8,128)} %get-tuple-element.17.med, s32[256,128]{1,0:T(8,128)} %get-tuple-element.18.info, s32[8,256]{1,0:T(8,128)} %get-tuple-element.19.across, ...), custom_call_target="tpu_custom_call" | custom-call | flops 3000000000 | bytes 16000000 | tf_op jit(solution)/shard_map/finish/pallas_call | solution.py:770

commit v4 on v3

--- a/solution.py
+++ b/solution.py
@@ -472,13 +472,19 @@
         hits = [spot == ramp[g * 16 : (g + 1) * 16] for g in range(first, first + 8)]
         return jnp.concatenate([jnp.where(hit, sign, jnp.zeros_like(sign)) for hit in hits], axis=0)
 
-    def sketch(k, work):
-        step = 4
+    def sketch(k, work, midway=()):
+        step = 8
         per = NB // 512
         used = sorted({j for j, _ in work if j is not None})
 
         def run(*sums):
             def chunk(t, carry):
+                for action, p in midway:
+
+                    @pl.when(t == 1)
+                    def _(action=action, p=p):
+                        action(p)
+
                 first = [unit * per + t * step for unit in (0, 1)]
 
                 def tile(unit, i):
@@ -600,6 +606,14 @@
             a_copy(p, d).wait_recv()
         e_copy(p).start()
 
+    def piece_out(p):
+        at = pl.ds(*PIECES[p])
+        return pltpu.make_async_copy(tot.at[at], table_ref.at[at], lsem.at[4 + p])
+
+    def e_finish(p):
+        e_copy(p).wait_recv()
+        piece_out(p).start()
+
     passes = (whole(0, 1), whole(2, 3), whole(4) + [(None, 0), (None, 1)])
     loads[2].wait()
     for p in range(3):
@@ -608,29 +622,27 @@
     loads[3].wait()
     sketch(0, passes[0])
     x_near_start(0)
-    sketch(0, passes[1])
+    sketch(0, passes[1], [(y_start, 0)])
     x_near_start(1)
-    y_start(0)
-    sketch(0, passes[2])
+    a_start(0)
+    sketch(0, passes[2], [(y_start, 1), (e_start, 0)])
     x_near_start(2)
-    a_start(0)
-    y_start(1)
+    a_start(1)
+    e_finish(0)
     y_start(2)
-    a_start(1)
+    e_start(1)
     a_start(2)
-    for p in range(3):
-        e_start(p)
-    for p in range(3):
-        e_copy(p).wait_recv()
-    result = pltpu.make_async_copy(tot, table_ref, lsem.at[4])
-    result.start()
+    e_finish(1)
+    e_start(2)
+    e_finish(2)
 
     for p in range(3):
         for copy in x_far[p] + [y_copy(p, d) for d in (1, 2, 3)] + [a_copy(p, d) for d in (1, 2, 3)] + [e_copy(p)]:
             copy.wait_send()
     on_core(0, *[copy.wait_send for copy in x_home])
     on_core(1, *[c.wait_send for p in range(3) for c in x_near[p]])
-    result.wait()
+    for p in range(3):
+        piece_out(p).wait()
 
 
 def run_main(*args):
@@ -697,7 +709,7 @@
             pltpu.VMEM((TAB // 2, 128), BF16),
             pltpu.VMEM((3, TAB // 8, 128), BF16),
             pltpu.VMEM((TAB, 128), F32),
-            dma((5,)), dma((2, 3, 2)), dma((4, 3)), dma((3, 3)), dma((3, 3)), dma((3, 4)), dma((3, 4)),
+            dma((7,)), dma((2, 3, 2)), dma((4, 3)), dma((3, 3)), dma((3, 3)), dma((3, 4)), dma((3, 4)),
         ],
         compiler_params=pltpu.CompilerParams(
             collective_id=1, has_side_effects=True, vmem_limit_bytes=62 * 1024 * 1024
@@ -712,9 +724,8 @@
     win_new, wout_new, mom_new, err_new,
     tabv, medv, infov, acrossv, momv, errv, winv, woutv, winn, woutn, momn, errn, sem, out_sem,
 ):
-    pairs = [(info, infov), (med, medv), (table, tabv), (across, acrossv), (w_in, winv), (w_out, woutv)]
-    for j in range(ROWS):
-        pairs += [(mom.at[:, j, :], momv.at[j]), (err.at[:, j, :], errv.at[j])]
+    pairs = [(mom.at[:, j, :], momv.at[j]) for j in range(ROWS)] + [(err.at[:, j, :], errv.at[j]) for j in range(ROWS)]
+    pairs += [(table, tabv), (info, infov), (med, medv), (across, acrossv), (w_in, winv), (w_out, woutv)]
     loads = [pltpu.make_async_copy(src, dst, sem.at[n]) for n, (src, dst) in enumerate(pairs)]
     for load in loads:
         load.start()
@@ -724,11 +735,21 @@
         stores.append(pltpu.make_async_copy(src, dst, out_sem.at[len(stores)]))
         stores[-1].start()
 
-    for load in loads[:4]:
+    loads[10].wait()
+    for j in range(ROWS):
+        loads[j].wait()
+        momn[j] = DECAY * momv[j] + tabv[j * COUNT : (j + 1) * COUNT, :]
+        store(momn.at[j], mom_new.at[:, j, :])
+    for load in loads[11:14]:
         load.wait()
     codes = infov[...]
     update = medv[...] + LEARN * tabv[LISTED:, :]
     kept = split2(jnp.where(codes[:, ROWS : ROWS + 1] == 1, update, 0.0))
+    for j in range(ROWS):
+        loads[5 + j].wait()
+        gone = tn(signed_hit(codes[:, j : j + 1]), kept)
+        errn[j] = errv[j] + LEARN * momn[j] - (gone[:, :128] + gone[:, 128:])
+        store(errn.at[j], err_new.at[:, j, :])
     places = acrossv[0:1, :]
 
     def delta(start, rows):
@@ -736,29 +757,20 @@
         got = nn(hit, kept)
         return got[:, :128] + got[:, 128:]
 
-    loads[4].wait()
+    loads[14].wait()
     for c in range(4):
         rows = pl.ds(c * 512, 512)
         for h in range(2):
             at = slice(h * 128, (h + 1) * 128)
             winn[rows, at] = winv[rows, at].astype(F32) - delta(h * 2048 + c * 512, 512)
         store(winn.at[rows], win_new.at[rows])
-    loads[5].wait()
+    loads[15].wait()
     for c in range(4):
         for q in range(4 * c, 4 * c + 4):
             at = slice(q * 128, (q + 1) * 128)
             woutn[:, at] = woutv[:, at].astype(F32) - delta(4096 + q * 256, 256)
         at = pl.ds(c * 512, 512)
         store(woutn.at[:, at], wout_new.at[:, at])
-    for j in range(ROWS):
-        loads[6 + 2 * j].wait()
-        loads[7 + 2 * j].wait()
-        fresh = DECAY * momv[j] + tabv[j * COUNT : (j + 1) * COUNT, :]
-        momn[j] = fresh
-        store(momn.at[j], mom_new.at[:, j, :])
-        gone = tn(signed_hit(codes[:, j : j + 1]), kept)
-        errn[j] = errv[j] + LEARN * fresh - (gone[:, :128] + gone[:, 128:])
-        store(errn.at[j], err_new.at[:, j, :])
     for copy in stores:
         copy.wait()
 

time: 140 us -> 144 us (1.029)
  Pallas kernels: 139 us -> 143 us
    pallas_call x1, Pallas kernels: 48.4 us -> 51.5 us  [run_sketch(): pl.pallas_call(sketch_kernel, out_shape=jax.ShapeDtypeStruct((TAB, 128),...]
where the time goes in v4:
time: 144 us
  Pallas kernels  143 us (99%)
  between operations  1.48 us (1%)
    pallas_call x1, Pallas kernels, run_main(): pl.pallas_call(main_kernel, out_shape=(jax.ShapeDtypeStruct((2, NB, 256),...  84.1 us
    pallas_call x1, Pallas kernels, run_sketch(): pl.pallas_call(sketch_kernel, out_shape=jax.ShapeDtypeStruct((TAB, 128),...  51.5 us
    pallas_call x1, Pallas kernels, run_finish(): pl.pallas_call(finish_kernel, out_shape=(jax.ShapeDtypeStruct(w_in.shape,...  7.25 us

profile of v4, /device:TPU:1, one launch (start us, length us, event | category | flops | bytes accessed | tf_op | source)
XLA Modules:
  0.0 144.4 jit_solution(16602732215278951706)
XLA Ops:
  1.3 84.1 %gather_grad.1 = (bf16[2,8192,256]{2,1,0:T(8,128)(2,1)}, s32[2,384,128]{2,1,0:T(8,128)}, s32[2,256,128]{2,1,0:T(8,128)}, f32[256,128]{1,0:T(8,128)}, s32[256,128]{1,0:T(8,128)}, /*index=5*/s32[8,256]{1,0:T(8,128)}) custom-call(bf16[104,2048]{1,0:T(8,128)(2,1)} %tok_ref.1, bf16[104,2048]{1,0:T(8,128)(2,1)} %cot_ref.1, bf16[2048,256]{1,0:T(8,128)(2,1)} %w_in.1, ...), custom_call_target="tpu_custom_call" | custom-call | flops 15000000512 | bytes 20000000 | tf_op jit(solution)/shard_map/gather_grad/pallas_call | solution.py:651
  85.4 51.5 %sketch_reduce.1.table = f32[2816,128]{1,0:T(8,128)} custom-call(bf16[2,8192,256]{2,1,0:T(8,128)(2,1)} %get-tuple-element.14.ghl_ref, s32[2,384,128]{2,1,0:T(8,128)} %get-tuple-element.15.codes_ref, s32[2,256,128]{2,1,0:T(8,128)} %get-tuple-element.16.spots_ref), custom_call_target="tpu_custom_call" | custom-call | flops 24000000000 | bytes 10000000 | tf_op jit(solution)/shard_map/sketch_reduce/pallas_call | solution.py:698
  137.0 7.3 %finish.1 = (f32[2048,256]{1,0:T(8,128)}, f32[256,2048]{1,0:T(8,128)}, f32[512,5,128]{2,1,0:T(8,128)}, f32[512,5,128]{2,1,0:T(8,128)}) custom-call(f32[2816,128]{1,0:T(8,128)} %sketch_reduce.1.table, f32[256,128]{1,0:T(8,128)} %get-tuple-element.17.med, s32[256,128]{1,0:T(8,128)} %get-tuple-element.18.info, s32[8,256]{1,0:T(8,128)} %get-tuple-element.19.across, ...), custom_call_target="tpu_custom_call" | custom-call | flops 3000000000 | bytes 16000000 | tf_op jit(solution)/shard_map/finish/pallas_call | solution.py:782

commit v5 on v3

--- a/solution.py
+++ b/solution.py
@@ -341,63 +341,68 @@
     out_last = pltpu.make_async_copy(ghl.at[:, pl.ds(4096, 4096)], ghl_ref.at[:, pl.ds(4096, 4096)], lsem.at[20])
     ready += [out_first, out_last]
 
-    def work(start, count, last=False):
-        rows = pl.ds(start, count)
+    def work(i, carry):
+        @pl.when(i == 0)
+        def _():
+            wait_sibling(0, 1, 2, 3)
+
+        @pl.when(i == 2)
+        def _():
+            arrive(2, 1)
+
+        @pl.when(i == 4)
+        def _():
+            wait_sibling(4)
+            arrive(3, 0)
+
+        @pl.when(i == 5)
+        def _():
+            wait_sibling(5)
+
+        @pl.when(i == 6)
+        def _():
+            arrive(3, 1)
+            wait_sibling(6)
+
+        @pl.when(i == 7)
+        def _():
+            ring(0, 3, 0).wait_recv()
+            sibling(7, 0).start()
+            ring(1, 3, 1).wait_recv()
+            sibling(7, 1).start()
+            wait_sibling(7)
+
+        rows = pl.ds(pl.multiple_of(i * CHIP, 16), CHIP)
         value, slope = gelu_pair(nn(buf[0, rows, :], wi[...]))
         back = nt(buf[1, rows, :], wo[...])
         hidden = value.astype(BF16)
         grad = (back * slope).astype(BF16)
         for c in range(4):
             at = slice(c * 512, (c + 1) * 512)
-            total = gin[at, :] + tn(buf[0, rows, at], grad)
-            if not last:
-                gin[at, :] = total
-                continue
-            for k in range(2):
-                for h in range(2):
-                    part = total[:, k * COLS + h * 128 : k * COLS + (h + 1) * 128]
-                    ghl[k, h * 2048 + c * 512 : h * 2048 + (c + 1) * 512, :] = split2(part)
-        if last:
-            out_first.start()
-        for c in range(4):
-            at = slice(c * 512, (c + 1) * 512)
-            total = gout[:, at] + tn(hidden, buf[1, rows, at])
-            if not last:
-                gout[:, at] = total
-                continue
-            for k in range(2):
-                for q in range(4 * c, 4 * c + 4):
-                    part = total[k * COLS : (k + 1) * COLS, (q - 4 * c) * 128 : (q - 4 * c + 1) * 128]
-                    ghl[k, 4096 + q * 256 : 4352 + q * 256, :] = split2(part)
-
-    def work_pair(i, carry):
-        @pl.when(i == 0)
-        def _():
-            wait_sibling(0, 1)
-
-        @pl.when(i == 1)
-        def _():
-            wait_sibling(2, 3)
-
-        @pl.when(i == 2)
-        def _():
-            arrive(2, 1)
-            arrive(3, 0)
-            wait_sibling(4, 5)
-
-        work(pl.multiple_of(i * (2 * CHIP), 16), 2 * CHIP)
+            gin[at, :] += tn(buf[0, rows, at], grad)
+            gout[:, at] += tn(hidden, buf[1, rows, at])
         return carry
 
-    lax.fori_loop(0, 3, work_pair, 0)
-    arrive(3, 1)
-    wait_sibling(6)
-    work(6 * CHIP, CHIP)
-    ring(0, 3, 0).wait_recv()
-    sibling(7, 0).start()
-    ring(1, 3, 1).wait_recv()
-    sibling(7, 1).start()
-    wait_sibling(7)
-    work(7 * CHIP, CHIP, last=True)
+    lax.fori_loop(0, NZ, work, 0)
+
+    def split_in(r, carry):
+        rows = pl.ds(pl.multiple_of(r * 256, 256), 256)
+        for k in range(2):
+            for h in range(2):
+                at = slice(k * COLS + h * 128, k * COLS + (h + 1) * 128)
+                ghl[k, pl.ds(pl.multiple_of(h * 2048 + r * 256, 256), 256), :] = split2(gin[rows, at])
+        return carry
+
+    def split_out(q, carry):
+        at = pl.ds(pl.multiple_of(q * 128, 128), 128)
+        for k in range(2):
+            rows = pl.ds(pl.multiple_of(4096 + q * 256, 256), 256)
+            ghl[k, rows, :] = split2(gout[k * COLS : (k + 1) * COLS, at])
+        return carry
+
+    lax.fori_loop(0, 8, split_in, 0)
+    out_first.start()
+    lax.fori_loop(0, 16, split_out, 0)
     out_last.start()
 
     for copy in list_copies + [w_in_first, w_out_first, meta_first]:
@@ -472,28 +477,32 @@
         hits = [spot == ramp[g * 16 : (g + 1) * 16] for g in range(first, first + 8)]
         return jnp.concatenate([jnp.where(hit, sign, jnp.zeros_like(sign)) for hit in hits], axis=0)
 
-    def sketch(k, work):
-        step = 4
+    def sketch(k, work, midway):
         per = NB // 512
         used = sorted({j for j, _ in work if j is not None})
 
         def run(*sums):
+            def push(unit, index, register):
+                at = pl.ds(pl.multiple_of((unit * per + index) * 256, 256), 256)
+                pltpu.matmul_push_rhs(ghl[k, at, :], register, unit)
+
             def chunk(t, carry):
-                first = [unit * per + t * step for unit in (0, 1)]
-
-                def tile(unit, i):
-                    return ghl[k, pl.ds(pl.multiple_of((first[unit] + i) * 256, 256), 256), :]
-
-                found = [
-                    {j: codes[k, pl.ds(pl.multiple_of(j * 64 + 2 * first[unit], 8), 2 * step), :] for j in used}
+                @pl.when(t == 3)
+                def _():
+                    midway()
+
+                wide = [
+                    {
+                        j: codes[k, pl.ds(pl.multiple_of(j * 64 + 2 * unit * per + (t // 2) * 8, 8), 8), :]
+                        for j in used
+                    }
                     for unit in (0, 1)
                 ]
-                for unit in (0, 1):
-                    pltpu.matmul_push_rhs(tile(unit, 0), 0, unit)
-                for i in range(step):
-                    if i + 1 < step:
-                        for unit in (0, 1):
-                            pltpu.matmul_push_rhs(tile(unit, i + 1), (i + 1) % 2, unit)
+                odd = lax.rem(t, 2) == 1
+                found = [{j: jnp.where(odd, v[4:8], v[0:4]) for j, v in each.items()} for each in wide]
+                for i in (0, 1):
+                    for unit in (0, 1):
+                        push(unit, 2 * t + 1 if i == 0 else lax.rem(2 * t + 2, per), 1 - i)
                     rows = [
                         {j: [spread(found[unit][j][2 * i + n : 2 * i + n + 1, :]) for n in (0, 1)] for j in used}
                         for unit in (0, 1)
@@ -501,7 +510,7 @@
                     for c, (j, q) in enumerate(work):
                         for unit in (0, 1):
                             if j is None:
-                                spot = spots[k, q * 128 : (q + 1) * 128, :] - (first[unit] + i) * 256
+                                spot = spots[k, q * 128 : (q + 1) * 128, :] - (unit * per + 2 * t + i) * 256
                                 lane = iota((128, 128), 1)
                                 hot = [jnp.where(spot == lane + 128 * n, 1.0, 0.0).astype(BF16) for n in (0, 1)]
                             else:
@@ -509,11 +518,15 @@
                             pltpu.matmul_acc_lhs(
                                 sums[2 * c + unit],
                                 jnp.concatenate(hot, axis=1),
-                                load_staged_rhs=i % 2 if c == 0 else None,
+                                load_staged_rhs=i if c == 0 else None,
                             )
                 return carry
 
-            lax.fori_loop(0, per // step, chunk, 0)
+            for unit in (0, 1):
+                push(unit, 0, 0)
+            lax.fori_loop(0, per // 2, chunk, 0)
+            for unit in (0, 1):
+                pltpu.matmul_acc_lhs(sums[unit], jnp.zeros((128, 256), BF16), load_staged_rhs=0)
             for c, (j, q) in enumerate(work):
                 total = pltpu.matmul_pop(sums[2 * c]) + pltpu.matmul_pop(sums[2 * c + 1])
                 start = q * 128 + (LISTED if j is None else j * COUNT)
@@ -600,37 +613,61 @@
             a_copy(p, d).wait_recv()
         e_copy(p).start()
 
+    def piece_out(p):
+        at = pl.ds(*PIECES[p])
+        return pltpu.make_async_copy(tot.at[at], table_ref.at[at], lsem.at[4 + p])
+
+    def e_finish(p):
+        e_copy(p).wait_recv()
+        piece_out(p).start()
+
     passes = (whole(0, 1), whole(2, 3), whole(4) + [(None, 0), (None, 1)])
+    midway = ((), ((y_start, 0),), ((y_start, 1), (e_start, 0)))
     loads[2].wait()
-    for p in range(3):
-        sketch(1, passes[p])
-        x_far_start(p)
-    loads[3].wait()
-    sketch(0, passes[0])
-    x_near_start(0)
-    sketch(0, passes[1])
-    x_near_start(1)
-    y_start(0)
-    sketch(0, passes[2])
-    x_near_start(2)
-    a_start(0)
-    y_start(1)
+
+    def shard_pass(turn, carry):
+        @pl.when(turn == 1)
+        def _():
+            loads[3].wait()
+
+        for p in range(3):
+
+            def between(p=p):
+                @pl.when(turn == 1)
+                def _():
+                    for action, piece in midway[p]:
+                        action(piece)
+
+            sketch(1 - turn, passes[p], between)
+
+            @pl.when(turn == 0)
+            def _(p=p):
+                x_far_start(p)
+
+            @pl.when(turn == 1)
+            def _(p=p):
+                x_near_start(p)
+                if p > 0:
+                    a_start(p - 1)
+
+        return carry
+
+    lax.fori_loop(0, 2, shard_pass, 0)
+    e_finish(0)
     y_start(2)
-    a_start(1)
+    e_start(1)
     a_start(2)
-    for p in range(3):
-        e_start(p)
-    for p in range(3):
-        e_copy(p).wait_recv()
-    result = pltpu.make_async_copy(tot, table_ref, lsem.at[4])
-    result.start()
+    e_finish(1)
+    e_start(2)
+    e_finish(2)
 
     for p in range(3):
         for copy in x_far[p] + [y_copy(p, d) for d in (1, 2, 3)] + [a_copy(p, d) for d in (1, 2, 3)] + [e_copy(p)]:
             copy.wait_send()
     on_core(0, *[copy.wait_send for copy in x_home])
     on_core(1, *[c.wait_send for p in range(3) for c in x_near[p]])
-    result.wait()
+    for p in range(3):
+        piece_out(p).wait()
 
 
 def run_main(*args):
@@ -697,7 +734,7 @@
             pltpu.VMEM((TAB // 2, 128), BF16),
             pltpu.VMEM((3, TAB // 8, 128), BF16),
             pltpu.VMEM((TAB, 128), F32),
-            dma((5,)), dma((2, 3, 2)), dma((4, 3)), dma((3, 3)), dma((3, 3)), dma((3, 4)), dma((3, 4)),
+            dma((7,)), dma((2, 3, 2)), dma((4, 3)), dma((3, 3)), dma((3, 3)), dma((3, 4)), dma((3, 4)),
         ],
         compiler_params=pltpu.CompilerParams(
             collective_id=1, has_side_effects=True, vmem_limit_bytes=62 * 1024 * 1024

time: 140 us -> 148 us (1.057)
  Pallas kernels: 139 us -> 147 us
    pallas_call x1, Pallas kernels: 48.4 us -> 52.7 us  [run_sketch(): pl.pallas_call(sketch_kernel, out_shape=jax.ShapeDtypeStruct((TAB, 128),...]
    pallas_call x1, Pallas kernels: 84.1 us -> 87.6 us  [run_main(): pl.pallas_call(main_kernel, out_shape=(jax.ShapeDtypeStruct((2, NB, 256),...]
where the time goes in v5:
time: 148 us
  Pallas kernels  147 us (99%)
    pallas_call x1, Pallas kernels, run_main(): pl.pallas_call(main_kernel, out_shape=(jax.ShapeDtypeStruct((2, NB, 256),...  87.6 us
    pallas_call x1, Pallas kernels, run_sketch(): pl.pallas_call(sketch_kernel, out_shape=jax.ShapeDtypeStruct((TAB, 128),...  52.7 us
    pallas_call x1, Pallas kernels, run_finish(): pl.pallas_call(finish_kernel, out_shape=(jax.ShapeDtypeStruct(w_in.shape,...  6.41 us

profile of v5, /device:TPU:1, one launch (start us, length us, event | category | flops | bytes accessed | tf_op | source)
XLA Modules:
  0.0 148.0 jit_solution(1021476862400502461)
XLA Ops:
  1.3 87.6 %gather_grad.1 = (bf16[2,8192,256]{2,1,0:T(8,128)(2,1)}, s32[2,384,128]{2,1,0:T(8,128)}, s32[2,256,128]{2,1,0:T(8,128)}, f32[256,128]{1,0:T(8,128)}, s32[256,128]{1,0:T(8,128)}, /*index=5*/s32[8,256]{1,0:T(8,128)}) custom-call(bf16[104,2048]{1,0:T(8,128)(2,1)} %tok_ref.1, bf16[104,2048]{1,0:T(8,128)(2,1)} %cot_ref.1, bf16[2048,256]{1,0:T(8,128)(2,1)} %w_in.1, ...), custom_call_target="tpu_custom_call" | custom-call | flops 15000000512 | bytes 20000000 | tf_op jit(solution)/shard_map/gather_grad/pallas_call | solution.py:676
  88.9 52.7 %sketch_reduce.1.table = f32[2816,128]{1,0:T(8,128)} custom-call(bf16[2,8192,256]{2,1,0:T(8,128)(2,1)} %get-tuple-element.14.ghl_ref, s32[2,384,128]{2,1,0:T(8,128)} %get-tuple-element.15.codes_ref, s32[2,256,128]{2,1,0:T(8,128)} %get-tuple-element.16.spots_ref), custom_call_target="tpu_custom_call" | custom-call | flops 24000000000 | bytes 10000000 | tf_op jit(solution)/shard_map/sketch_reduce/pallas_call | solution.py:723
  141.6 6.4 %finish.1 = (f32[2048,256]{1,0:T(8,128)}, f32[256,2048]{1,0:T(8,128)}, f32[512,5,128]{2,1,0:T(8,128)}, f32[512,5,128]{2,1,0:T(8,128)}) custom-call(f32[2816,128]{1,0:T(8,128)} %sketch_reduce.1.table, f32[256,128]{1,0:T(8,128)} %get-tuple-element.17.med, s32[256,128]{1,0:T(8,128)} %get-tuple-element.18.info, s32[8,256]{1,0:T(8,128)} %get-tuple-element.19.across, ...), custom_call_target="tpu_custom_call" | custom-call | flops 3000000000 | bytes 16000000 | tf_op jit(solution)/shard_map/finish/pallas_call | solution.py:807

commit v6 on v3

--- a/solution.py
+++ b/solution.py
@@ -600,37 +600,49 @@
             a_copy(p, d).wait_recv()
         e_copy(p).start()
 
+    def piece_out(p):
+        at = pl.ds(*PIECES[p])
+        return pltpu.make_async_copy(tot.at[at], table_ref.at[at], lsem.at[4 + p])
+
+    def e_finish(p):
+        e_copy(p).wait_recv()
+        piece_out(p).start()
+
     passes = (whole(0, 1), whole(2, 3), whole(4) + [(None, 0), (None, 1)])
     loads[2].wait()
-    for p in range(3):
-        sketch(1, passes[p])
-        x_far_start(p)
+    sketch(1, passes[0])
+    x_far_start(0)
     loads[3].wait()
     sketch(0, passes[0])
     x_near_start(0)
+    sketch(1, passes[1])
+    x_far_start(1)
+    y_start(0)
     sketch(0, passes[1])
     x_near_start(1)
-    y_start(0)
+    a_start(0)
+    sketch(1, passes[2])
+    x_far_start(2)
+    y_start(1)
+    e_start(0)
     sketch(0, passes[2])
     x_near_start(2)
-    a_start(0)
-    y_start(1)
+    a_start(1)
+    e_finish(0)
     y_start(2)
-    a_start(1)
+    e_start(1)
     a_start(2)
-    for p in range(3):
-        e_start(p)
-    for p in range(3):
-        e_copy(p).wait_recv()
-    result = pltpu.make_async_copy(tot, table_ref, lsem.at[4])
-    result.start()
+    e_finish(1)
+    e_start(2)
+    e_finish(2)
 
     for p in range(3):
         for copy in x_far[p] + [y_copy(p, d) for d in (1, 2, 3)] + [a_copy(p, d) for d in (1, 2, 3)] + [e_copy(p)]:
             copy.wait_send()
     on_core(0, *[copy.wait_send for copy in x_home])
     on_core(1, *[c.wait_send for p in range(3) for c in x_near[p]])
-    result.wait()
+    for p in range(3):
+        piece_out(p).wait()
 
 
 def run_main(*args):
@@ -697,7 +709,7 @@
             pltpu.VMEM((TAB // 2, 128), BF16),
             pltpu.VMEM((3, TAB // 8, 128), BF16),
             pltpu.VMEM((TAB, 128), F32),
-            dma((5,)), dma((2, 3, 2)), dma((4, 3)), dma((3, 3)), dma((3, 3)), dma((3, 4)), dma((3, 4)),
+            dma((7,)), dma((2, 3, 2)), dma((4, 3)), dma((3, 3)), dma((3, 3)), dma((3, 4)), dma((3, 4)),
         ],
         compiler_params=pltpu.CompilerParams(
             collective_id=1, has_side_effects=True, vmem_limit_bytes=62 * 1024 * 1024

time: 140 us -> 139 us (level)
  no operation moved by 1% of the time
where the time goes in v6:
time: 139 us
  Pallas kernels  138 us (99%)
  between operations  1.48 us (1%)
    pallas_call x1, Pallas kernels, run_main(): pl.pallas_call(main_kernel, out_shape=(jax.ShapeDtypeStruct((2, NB, 256),...  84.1 us
    pallas_call x1, Pallas kernels, run_sketch(): pl.pallas_call(sketch_kernel, out_shape=jax.ShapeDtypeStruct((TAB, 128),...  47.3 us
    pallas_call x1, Pallas kernels, run_finish(): pl.pallas_call(finish_kernel, out_shape=(jax.ShapeDtypeStruct(w_in.shape,...  6.42 us

profile of v6, /device:TPU:1, one launch (start us, length us, event | category | flops | bytes accessed | tf_op | source)
XLA Modules:
  0.0 139.3 jit_solution(3891460710536734864)
XLA Ops:
  1.3 84.1 %gather_grad.1 = (bf16[2,8192,256]{2,1,0:T(8,128)(2,1)}, s32[2,384,128]{2,1,0:T(8,128)}, s32[2,256,128]{2,1,0:T(8,128)}, f32[256,128]{1,0:T(8,128)}, s32[256,128]{1,0:T(8,128)}, /*index=5*/s32[8,256]{1,0:T(8,128)}) custom-call(bf16[104,2048]{1,0:T(8,128)(2,1)} %tok_ref.1, bf16[104,2048]{1,0:T(8,128)(2,1)} %cot_ref.1, bf16[2048,256]{1,0:T(8,128)(2,1)} %w_in.1, ...), custom_call_target="tpu_custom_call" | custom-call | flops 15000000512 | bytes 20000000 | tf_op jit(solution)/shard_map/gather_grad/pallas_call | solution.py:651
  85.4 47.3 %sketch_reduce.1.table = f32[2816,128]{1,0:T(8,128)} custom-call(bf16[2,8192,256]{2,1,0:T(8,128)(2,1)} %get-tuple-element.14.ghl_ref, s32[2,384,128]{2,1,0:T(8,128)} %get-tuple-element.15.codes_ref, s32[2,256,128]{2,1,0:T(8,128)} %get-tuple-element.16.spots_ref), custom_call_target="tpu_custom_call" | custom-call | flops 24000000000 | bytes 10000000 | tf_op jit(solution)/shard_map/sketch_reduce/pallas_call | solution.py:698
  132.7 6.4 %finish.1 = (f32[2048,256]{1,0:T(8,128)}, f32[256,2048]{1,0:T(8,128)}, f32[512,5,128]{2,1,0:T(8,128)}, f32[512,5,128]{2,1,0:T(8,128)}) custom-call(f32[2816,128]{1,0:T(8,128)} %sketch_reduce.1.table, f32[256,128]{1,0:T(8,128)} %get-tuple-element.17.med, s32[256,128]{1,0:T(8,128)} %get-tuple-element.18.info, s32[8,256]{1,0:T(8,128)} %get-tuple-element.19.across, ...), custom_call_target="tpu_custom_call" | custom-call | flops 3000000000 | bytes 16000000 | tf_op jit(solution)/shard_map/finish/pallas_call | solution.py:782

commit v7 on v6

--- a/solution.py
+++ b/solution.py
@@ -231,6 +231,41 @@
     on_core(0, w_in_first.start, w_out_first.start, own_wi.start, own_wo.start)
     on_core(1, w_out_first.start, w_in_first.start)
 
+    on_core(0, own_tok.wait, give_cot.wait)
+    on_core(1, own_cot.wait, give_tok.wait)
+    for c in range(4):
+        at = slice(c * 512, (c + 1) * 512)
+        mine, theirs = own[:, at].astype(F32), land[:, at].astype(F32)
+        first, second = jnp.where(core == 0, mine, theirs), jnp.where(core == 0, theirs, mine)
+        buf[core, 0:CHIP, at] = jnp.concatenate([first, second], axis=0).astype(BF16)
+
+    def turn_of(way, sub):
+        return sub if way == 0 else 1 - sub
+
+    def unit_of(hops, turn):
+        return 0 if hops == 0 else 2 * hops - 1 + turn
+
+    def rows_of(unit, sub):
+        return pl.ds(unit * CHIP + SUBS[sub][0], SUBS[sub][1])
+
+    def ring(way, hops, sub):
+        turn = turn_of(way, sub)
+        return remote(
+            buf.at[core, rows_of(unit_of(hops, turn), sub)],
+            buf.at[core, rows_of(unit_of(hops + 1, turn), sub)],
+            ring_s.at[way, hops, sub], ring_r.at[way, hops, sub],
+            dev(dz=1 if way == 0 else -1),
+        )
+
+    def sibling(unit, sub):
+        at = buf.at[core, rows_of(unit, sub)]
+        return remote(at, at, sib_s.at[unit, sub], sib_r.at[unit, sub], dev(to=other))
+
+    for turn in (0, 1):
+        ring(0, 0, turn).start()
+        ring(1, 0, 1 - turn).start()
+    for sub in (0, 1):
+        sibling(0, sub).start()
     loads[0].wait()
     listed = jnp.concatenate([lstv[...], jnp.full(lstv.shape, cnt_ref[0, 0], I32)], axis=1)
     meta[pl.ds(pl.multiple_of(CODE + 8 * rep, 8), 8), :] = jnp.where(iota((8, 128), 0) == rep, listed, 0)
@@ -241,41 +276,6 @@
     for copy in list_copies:
         copy.start()
 
-    on_core(0, own_tok.wait, give_cot.wait)
-    on_core(1, own_cot.wait, give_tok.wait)
-    for c in range(4):
-        at = slice(c * 512, (c + 1) * 512)
-        mine, theirs = own[:, at].astype(F32), land[:, at].astype(F32)
-        first, second = jnp.where(core == 0, mine, theirs), jnp.where(core == 0, theirs, mine)
-        buf[core, 0:CHIP, at] = jnp.concatenate([first, second], axis=0).astype(BF16)
-
-    def turn_of(way, sub):
-        return sub if way == 0 else 1 - sub
-
-    def unit_of(hops, turn):
-        return 0 if hops == 0 else 2 * hops - 1 + turn
-
-    def rows_of(unit, sub):
-        return pl.ds(unit * CHIP + SUBS[sub][0], SUBS[sub][1])
-
-    def ring(way, hops, sub):
-        turn = turn_of(way, sub)
-        return remote(
-            buf.at[core, rows_of(unit_of(hops, turn), sub)],
-            buf.at[core, rows_of(unit_of(hops + 1, turn), sub)],
-            ring_s.at[way, hops, sub], ring_r.at[way, hops, sub],
-            dev(dz=1 if way == 0 else -1),
-        )
-
-    def sibling(unit, sub):
-        at = buf.at[core, rows_of(unit, sub)]
-        return remote(at, at, sib_s.at[unit, sub], sib_r.at[unit, sub], dev(to=other))
-
-    for turn in (0, 1):
-        ring(0, 0, turn).start()
-        ring(1, 0, 1 - turn).start()
-    for sub in (0, 1):
-        sibling(0, sub).start()
     for load in tables:
         load.start()
 
@@ -379,9 +379,12 @@
         def _():
             wait_sibling(2, 3)
 
+        @pl.when(i == 1)
+        def _():
+            arrive(2, 1)
+
         @pl.when(i == 2)
         def _():
-            arrive(2, 1)
             arrive(3, 0)
             wait_sibling(4, 5)
 
@@ -476,6 +479,7 @@
         step = 4
         per = NB // 512
         used = sorted({j for j, _ in work if j is not None})
+        rows_in = [64 if part == (None, 1) else 128 for part in work]
 
         def run(*sums):
             def chunk(t, carry):
@@ -501,8 +505,8 @@
                     for c, (j, q) in enumerate(work):
                         for unit in (0, 1):
                             if j is None:
-                                spot = spots[k, q * 128 : (q + 1) * 128, :] - (first[unit] + i) * 256
-                                lane = iota((128, 128), 1)
+                                spot = spots[k, q * 128 : q * 128 + rows_in[c], :] - (first[unit] + i) * 256
+                                lane = iota((rows_in[c], 128), 1)
                                 hot = [jnp.where(spot == lane + 128 * n, 1.0, 0.0).astype(BF16) for n in (0, 1)]
                             else:
                                 hot = [one_hot(rows[unit][j][n], q) for n in (0, 1)]
@@ -517,9 +521,9 @@
             for c, (j, q) in enumerate(work):
                 total = pltpu.matmul_pop(sums[2 * c]) + pltpu.matmul_pop(sums[2 * c + 1])
                 start = q * 128 + (LISTED if j is None else j * COUNT)
-                outb[k, start : start + 128, :] = (total[:, :128] + total[:, 128:]).astype(BF16)
-
-        pl.run_scoped(run, *[pltpu.ACC(mxu_id=unit)((128, 256), F32) for _ in work for unit in (0, 1)])
+                outb[k, start : start + rows_in[c], :] = (total[:, :128] + total[:, 128:]).astype(BF16)
+
+        pl.run_scoped(run, *[pltpu.ACC(mxu_id=unit)((rows, 256), F32) for rows in rows_in for unit in (0, 1)])
 
     def whole(*rows):
         return [(j, q) for j in rows for q in range(4)]
@@ -609,6 +613,8 @@
         piece_out(p).start()
 
     passes = (whole(0, 1), whole(2, 3), whole(4) + [(None, 0), (None, 1)])
+    for k in range(2):
+        outb[k, LISTED + 192 :, :] = jnp.zeros((LIVE - 192, 128), BF16)
     loads[2].wait()
     sketch(1, passes[0])
     x_far_start(0)

time: 139 us -> 141 us (1.014)
    pallas_call x1, Pallas kernels: 84.1 us -> 86.7 us  [run_main(): pl.pallas_call(main_kernel, out_shape=(jax.ShapeDtypeStruct((2, NB, 256),...]
where the time goes in v7:
time: 141 us
  Pallas kernels  139 us (99%)
  between operations  1.48 us (1%)
    pallas_call x1, Pallas kernels, run_main(): pl.pallas_call(main_kernel, out_shape=(jax.ShapeDtypeStruct((2, NB, 256),...  86.7 us
    pallas_call x1, Pallas kernels, run_sketch(): pl.pallas_call(sketch_kernel, out_shape=jax.ShapeDtypeStruct((TAB, 128),...  46.1 us
    pallas_call x1, Pallas kernels, run_finish(): pl.pallas_call(finish_kernel, out_shape=(jax.ShapeDtypeStruct(w_in.shape,...  6.42 us

profile of v7, /device:TPU:1, one launch (start us, length us, event | category | flops | bytes accessed | tf_op | source)
XLA Modules:
  0.0 140.7 jit_solution(752586722279686490)
XLA Ops:
  1.3 86.7 %gather_grad.1 = (bf16[2,8192,256]{2,1,0:T(8,128)(2,1)}, s32[2,384,128]{2,1,0:T(8,128)}, s32[2,256,128]{2,1,0:T(8,128)}, f32[256,128]{1,0:T(8,128)}, s32[256,128]{1,0:T(8,128)}, /*index=5*/s32[8,256]{1,0:T(8,128)}) custom-call(bf16[104,2048]{1,0:T(8,128)(2,1)} %tok_ref.1, bf16[104,2048]{1,0:T(8,128)(2,1)} %cot_ref.1, bf16[2048,256]{1,0:T(8,128)(2,1)} %w_in.1, ...), custom_call_target="tpu_custom_call" | custom-call | flops 15000000512 | bytes 20000000 | tf_op jit(solution)/shard_map/gather_grad/pallas_call | solution.py:657
  88.0 46.1 %sketch_reduce.1.table = f32[2816,128]{1,0:T(8,128)} custom-call(bf16[2,8192,256]{2,1,0:T(8,128)(2,1)} %get-tuple-element.14.ghl_ref, s32[2,384,128]{2,1,0:T(8,128)} %get-tuple-element.15.codes_ref, s32[2,256,128]{2,1,0:T(8,128)} %get-tuple-element.16.spots_ref), custom_call_target="tpu_custom_call" | custom-call | flops 24000000000 | bytes 10000000 | tf_op jit(solution)/shard_map/sketch_reduce/pallas_call | solution.py:704
  134.1 6.4 %finish.1 = (f32[2048,256]{1,0:T(8,128)}, f32[256,2048]{1,0:T(8,128)}, f32[512,5,128]{2,1,0:T(8,128)}, f32[512,5,128]{2,1,0:T(8,128)}) custom-call(f32[2816,128]{1,0:T(8,128)} %sketch_reduce.1.table, f32[256,128]{1,0:T(8,128)} %get-tuple-element.17.med, s32[256,128]{1,0:T(8,128)} %get-tuple-element.18.info, s32[8,256]{1,0:T(8,128)} %get-tuple-element.19.across, ...), custom_call_target="tpu_custom_call" | custom-call | flops 3000000000 | bytes 16000000 | tf_op jit(solution)/shard_map/finish/pallas_call | solution.py:788

commit v8 on v6

--- a/solution.py
+++ b/solution.py
@@ -166,7 +166,7 @@
     tok_ref, cot_ref, win_ref, wout_ref, ord_ref, sgn_ref, lst_ref, cnt_ref, mom_ref, err_ref,
     ghl_ref, codes_ref, spots_ref, med_ref, info_ref, across_ref,
     own, land, buf, wi, wo, gin, gout, ordv, sgnv, meta, meta2, ghl,
-    momv, errv, medv, infov, acrossv, spots, lstv,
+    momv, errv, medv, infov, acrossv, spots, lstv, early, late,
     lsem, land_sem, ring_s, ring_r, sib_s, sib_r, w_s, w_r, list_s, list_r, meta_s, meta_r,
 ):
     rep, shard = lax.axis_index("rep"), lax.axis_index("shard")
@@ -338,13 +338,29 @@
                 sibling(unit, sub).wait_recv()
 
     out_first = pltpu.make_async_copy(ghl.at[:, pl.ds(0, 4096)], ghl_ref.at[:, pl.ds(0, 4096)], lsem.at[19])
-    out_last = pltpu.make_async_copy(ghl.at[:, pl.ds(4096, 4096)], ghl_ref.at[:, pl.ds(4096, 4096)], lsem.at[20])
-    ready += [out_first, out_last]
+    out_next = [
+        pltpu.make_async_copy(ghl.at[:, pl.ds(start, 2048)], ghl_ref.at[:, pl.ds(start, 2048)], lsem.at[sem])
+        for start, sem in ((4096, 20), (6144, 23))
+    ]
+    ready += [out_first, *out_next]
 
     def work(start, count, last=False):
         rows = pl.ds(start, count)
-        value, slope = gelu_pair(nn(buf[0, rows, :], wi[...]))
-        back = nt(buf[1, rows, :], wo[...])
+        if last:
+            def product(kind, into):
+                into[...] = nn(buf[0, rows, :], wi[...]) if kind == 0 else nt(buf[1, rows, :], wo[...])
+
+            on_core(0, functools.partial(product, 0, early))
+            on_core(1, functools.partial(product, 1, early))
+            wait_sibling(7)
+            on_core(0, functools.partial(product, 1, late))
+            on_core(1, functools.partial(product, 0, late))
+            one, two = early[...], late[...]
+            value, slope = gelu_pair(jnp.where(core == 0, one, two))
+            back = jnp.where(core == 0, two, one)
+        else:
+            value, slope = gelu_pair(nn(buf[0, rows, :], wi[...]))
+            back = nt(buf[1, rows, :], wo[...])
         hidden = value.astype(BF16)
         grad = (back * slope).astype(BF16)
         for c in range(4):
@@ -369,6 +385,8 @@
                 for q in range(4 * c, 4 * c + 4):
                     part = total[k * COLS : (k + 1) * COLS, (q - 4 * c) * 128 : (q - 4 * c + 1) * 128]
                     ghl[k, 4096 + q * 256 : 4352 + q * 256, :] = split2(part)
+            if c % 2 == 1:
+                out_next[c // 2].start()
 
     def work_pair(i, carry):
         @pl.when(i == 0)
@@ -396,9 +414,7 @@
     sibling(7, 0).start()
     ring(1, 3, 1).wait_recv()
     sibling(7, 1).start()
-    wait_sibling(7)
     work(7 * CHIP, CHIP, last=True)
-    out_last.start()
 
     for copy in list_copies + [w_in_first, w_out_first, meta_first]:
         copy.wait_send()
@@ -680,7 +696,9 @@
             pltpu.VMEM((8, LIVE), I32),
             pltpu.VMEM((2, LIVE, 128), I32),
             pltpu.VMEM((1, 64), I32),
-            dma((23,)), dma((2,)),
+            pltpu.VMEM((CHIP, 2 * COLS), F32),
+            pltpu.VMEM((CHIP, 2 * COLS), F32),
+            dma((24,)), dma((2,)),
             dma((2, 4, 2)), dma((2, 4, 2)), dma((NZ, 2)), dma((NZ, 2)), dma((4,)), dma((4,)),
             dma((7,)), dma((7,)), dma((2,)), dma((2,)),
         ],

time: 139 us -> 139 us (level)
  no operation moved by 1% of the time
where the time goes in v8:
time: 139 us
  Pallas kernels  138 us (99%)
  between operations  1.48 us (1%)
    pallas_call x1, Pallas kernels, run_main(): pl.pallas_call(main_kernel, out_shape=(jax.ShapeDtypeStruct((2, NB, 256),...  84.9 us
    pallas_call x1, Pallas kernels, run_sketch(): pl.pallas_call(sketch_kernel, out_shape=jax.ShapeDtypeStruct((TAB, 128),...  46.3 us
    pallas_call x1, Pallas kernels, run_finish(): pl.pallas_call(finish_kernel, out_shape=(jax.ShapeDtypeStruct(w_in.shape,...  6.42 us

profile of v8, /device:TPU:1, one launch (start us, length us, event | category | flops | bytes accessed | tf_op | source)
XLA Modules:
  0.0 139.1 jit_solution(13254116487536072755)
XLA Ops:
  1.3 84.9 %gather_grad.1 = (bf16[2,8192,256]{2,1,0:T(8,128)(2,1)}, s32[2,384,128]{2,1,0:T(8,128)}, s32[2,256,128]{2,1,0:T(8,128)}, f32[256,128]{1,0:T(8,128)}, s32[256,128]{1,0:T(8,128)}, /*index=5*/s32[8,256]{1,0:T(8,128)}) custom-call(bf16[104,2048]{1,0:T(8,128)(2,1)} %tok_ref.1, bf16[104,2048]{1,0:T(8,128)(2,1)} %cot_ref.1, bf16[2048,256]{1,0:T(8,128)(2,1)} %w_in.1, ...), custom_call_target="tpu_custom_call" | custom-call | flops 15000000512 | bytes 20000000 | tf_op jit(solution)/shard_map/gather_grad/pallas_call | solution.py:667
  86.2 46.3 %sketch_reduce.1.table = f32[2816,128]{1,0:T(8,128)} custom-call(bf16[2,8192,256]{2,1,0:T(8,128)(2,1)} %get-tuple-element.14.ghl_ref, s32[2,384,128]{2,1,0:T(8,128)} %get-tuple-element.15.codes_ref, s32[2,256,128]{2,1,0:T(8,128)} %get-tuple-element.16.spots_ref), custom_call_target="tpu_custom_call" | custom-call | flops 24000000000 | bytes 10000000 | tf_op jit(solution)/shard_map/sketch_reduce/pallas_call | solution.py:716
  132.5 6.4 %finish.1 = (f32[2048,256]{1,0:T(8,128)}, f32[256,2048]{1,0:T(8,128)}, f32[512,5,128]{2,1,0:T(8,128)}, f32[512,5,128]{2,1,0:T(8,128)}) custom-call(f32[2816,128]{1,0:T(8,128)} %sketch_reduce.1.table, f32[256,128]{1,0:T(8,128)} %get-tuple-element.17.med, s32[256,128]{1,0:T(8,128)} %get-tuple-element.18.info, s32[8,256]{1,0:T(8,128)} %get-tuple-element.19.across, ...), custom_call_target="tpu_custom_call" | custom-call | flops 3000000000 | bytes 16000000 | tf_op jit(solution)/shard_map/finish/pallas_call | solution.py:800
